TPU v7x, 128 devices: a whole 4x4x4 slice. The times are simulated.
128 devices in a mesh: clip: 4 (over z), frame: 8 (over x, core), row: 4 (over y).
Axes of the slice: x: 4, y: 4, z: 4, core: 2. Of those that a mesh axis runs over, the one named last changes fastest.
Arguments:
- latents: bfloat16 [256, 16, 40, 512], P(('clip', 'frame'), 'row'), parts along dimension 0, may hold values from -12 to 12
- hidden: bfloat16 [256, 16, 40, 512], P(('clip', 'frame'), 'row'), parts along dimension 0, may hold values from -12 to 12
- norm_gain: float32 [512], replicated, may hold values from 0.1 to 1.9
- norm_bias: float32 [512], replicated, may hold values from -3 to 3
- conv_weight: bfloat16 [3, 3, 3, 512, 512], replicated, may hold values from -0.0546875 to 0.0546875
Outputs:
- block_out: bfloat16 [256, 16, 40, 512], P(('clip', 'frame'), 'row'), parts along dimension 0
There are 4 independent parts, one for each index of `clip`. A program takes and returns all parts, laid end to end along the dimension named above; an argument that names none is the same for every part. Nothing has to cross between parts.
All inputs are finite; a program needn't handle non-finite values.
Results may differ from a plain program's by a relative error of at most 0.0013.
The roundings to bfloat16 on the way count: a program that leaves them out, or rounds other values in their place, can miss the bound.
Values may be sent and summed in bfloat16 or wider, within the bound.
No kernel may reach another device: no remote copies, remote signals or barrier semaphores. Data moves between devices by JAX's collectives and lax.ppermute only.
A program may use at most 192 MiB of HBM per device.

v0:
```python
import jax
import jax.numpy as jnp
from jax import lax
from jax.sharding import PartitionSpec as P

GROUPS = 32


TAPS = [(p, q, r) for p in range(3) for q in range(3) for r in range(3)]


def from_behind(shard, axis, by):
    size = lax.axis_size(axis)
    pairs = [(i, i + by) for i in range(size) if 0 <= i + by < size]
    return lax.ppermute(shard, axis, pairs)


def unfold(padded, nframes, nrows, ncols):
    slabs = [padded[p : p + nframes, q : q + nrows, r : r + ncols] for p, q, r in TAPS]
    joined = jnp.concatenate(slabs, axis=-1)
    return joined.reshape(nframes * nrows * ncols, -1)


def time_padded(act):
    previous = from_behind(act[-2:], "frame", 1)
    first = jnp.concatenate([act[:1], act[:1]], axis=0)
    lead = jnp.where(lax.axis_index("frame") == 0, first, previous)
    return jnp.concatenate([lead, act], axis=0)


def convolve(act, weight):
    nframes, nrows, ncols, width = act.shape
    lead = time_padded(act)
    row_count = lax.axis_size("row")
    share = width // row_count
    offset = lax.axis_index("row") * share
    strips = lax.all_to_all(lead, "row", split_axis=3, concat_axis=1, tiled=True)
    weight_part = lax.dynamic_slice_in_dim(weight, offset, share, 3)
    padded = jnp.pad(strips, ((0, 0), (1, 1), (1, 1), (0, 0)))
    all_rows = nrows * row_count
    columns = unfold(padded, nframes, all_rows, ncols)
    partial_value = jnp.dot(
        columns, weight_part.reshape(-1, width), preferred_element_type=jnp.float32
    )
    partial_value = partial_value.reshape(nframes, all_rows, ncols, width)
    return lax.psum_scatter(partial_value, "row", scatter_dimension=1, tiled=True)


def normalize(values, gain, bias):
    width = values.shape[-1]
    members = width // GROUPS
    flat = values.astype(jnp.float32).reshape(-1, GROUPS, members)
    count = float(flat.shape[0] * members * lax.axis_size("frame") * lax.axis_size("row"))
    local_sum = jnp.sum(flat, axis=(0, 2))
    mean = lax.psum(local_sum, ("frame", "row")) / count
    centered = flat - mean[None, :, None]
    spread = lax.psum(jnp.sum(centered * centered, axis=(0, 2)), ("frame", "row")) / count
    normed = (flat - mean[None, :, None]) / jnp.sqrt(spread[None, :, None] + 1e-06)
    return normed.reshape(values.shape) * gain + bias


def shards(latents, hidden, norm_gain, norm_bias, conv_weight):
    act = jax.nn.silu(normalize(hidden, norm_gain, norm_bias)).astype(jnp.bfloat16)
    result = latents.astype(jnp.float32) + convolve(act, conv_weight)
    return result.astype(jnp.bfloat16)


def solution(mesh):
    in_specs = (
        P(("clip", "frame"), "row", None, None),
        P(("clip", "frame"), "row", None, None),
        P(),
        P(),
        P(),
    )
    out_specs = P(("clip", "frame"), "row", None, None)
    return jax.shard_map(shards, mesh=mesh, in_specs=in_specs, out_specs=out_specs, check_vma=False)
```

profile of v0, /device:TPU:1, one launch (start us, length us, event | category | flops | bytes accessed | tf_op | source)
XLA Modules:
  0.0 484.6 jit_solution(9291693929355736777)
XLA Ops:
  8.4 63.8 %psum.14 = f32[32]{0:T(128)S(1)} all-reduce(f32[32]{0:T(128)S(1)} %reduce_sum.25), channel_id=1, replica_groups=mesh['clip'=4,'frame'=8,'row'=4] {'frame','row'}, use_global_device_ids=true, to_apply=%region_2.0 | all-reduce | flops 32 | bytes 256 | tf_op jit(solution)/shard_map/psum | solution.py:55
  74.3 62.7 %psum.15 = f32[32]{0:T(128)S(1)} all-reduce(f32[32]{0:T(128)S(1)} %reduce_sum.37), channel_id=1, replica_groups=mesh['clip'=4,'frame'=8,'row'=4] {'frame','row'}, use_global_device_ids=true, to_apply=%region_5.6 | all-reduce | flops 32 | bytes 256 | tf_op jit(solution)/shard_map/psum | solution.py:57
  138.1 1.9 collective-permute-start
  140.1 5.5 %collective-permute-done = bf16[2,4,40,512]{3,2,1,0:T(8,128)(2,1)S(1)} collective-permute-done((bf16[2,4,40,512]{3,2,1,0:T(8,128)(2,1)S(1)}, bf16[2,4,40,512]{3,2,1,0:T(8,128)(2,1)S(1)}, u32[]{:S(2)}, u32[]{:S(2)}) %collective-permute-start) | collective-permute-done | bytes 327712 | tf_op jit(solution)/shard_map/ppermute | solution.py:15
  147.0 12.8 %copy.10 = bf16[10,4,40,512]{2,0,1,3:T(8,128)(2,1)} copy(bf16[10,4,40,512]{3,2,1,0:T(8,128)(2,1)} %pad_maximum_fusion) | data formatting | bytes 3276800 | tf_op jit(solution)/shard_map/concatenate | solution.py:28
  159.8 10.4 %reshape.28 = bf16[4,2,102400]{2,1,0:T(2,128)(2,1)} reshape(bf16[512,4,10,40]{3,2,1,0:T(8,128)(2,1)} %bitcast.48) | data formatting | bytes 3276800
  170.1 3.6 all-to-all-start
  173.8 4.2 constant_dynamic-slice_fusion
  178.0 17.1 %all-to-all-done = bf16[4,2,102400]{2,1,0:T(2,128)(2,1)S(1)} async-done(((bf16[4,2,102400]{2,1,0:T(2,128)(2,1)}), bf16[4,2,102400]{2,1,0:T(2,128)(2,1)S(1)}, u32[]{:S(2)}, u32[]{:S(2)}) %all-to-all-start) | async-done | bytes 1638432 | tf_op jit(solution)/shard_map/all_to_all | solution.py:37
  195.1 9.0 %reshape.29 = bf16[512,4,10,40]{3,2,1,0:T(8,128)(2,1)} reshape(bf16[4,2,102400]{2,1,0:T(2,128)(2,1)S(1)} %all-to-all-done) | data formatting | bytes 3276800
  204.1 8.8 %copy.11 = bf16[10,4,40,4,128]{4,2,1,3,0:T(8,128)(2,1)S(1)} copy(bf16[10,4,40,4,128]{2,0,1,4,3:T(8,128)(2,1)} %bitcast.49) | data formatting | bytes 3276800 | tf_op jit(solution)/shard_map/all_to_all | solution.py:37
  215.7 1.9 fusion.8
  217.6 1.8 fusion.9
  221.5 1.8 fusion.10
  230.8 1.8 fusion.16
  232.7 1.9 fusion.17
  235.8 1.8 fusion.18
  245.0 1.9 fusion.24
  249.9 1.8 fusion.26
  251.7 1.8 fusion.27
  254.8 1.7 fusion.29
  256.5 25.0 %fusion.31 = f32[8,16,40,512]{3,2,1,0:T(8,128)} fusion(bf16[8,16,40,3456]{3,2,1,0:T(8,128)(2,1)} %fusion.29, bf16[3456,512,1,1]{1,0,3,2:T(8,128)(2,1)S(1)} %bitcast.53), kind=kOutput, calls=%fused_computation.67 | convolution fusion | flops 18119393280 | bytes 49414144 | tf_op jit(solution)/shard_map/dot_general | solution.py:42
  283.4 191.1 %all-reduce.4.cloned.1.call-done = f32[8,16,40,512]{3,2,1,0:T(8,128)} async-done(((f32[8,16,40,512]{3,2,1,0:T(8,128)}), f32[8,16,40,512]{3,2,1,0:T(8,128)}) %all-reduce.4.cloned.1.call-update) | async-done | bytes 10485776
  474.5 3.2 fusion.5
  (50 shorter events, 33.2 us)
Async XLA Ops:
  6.5 130.6 %copy-start = (bf16[8,4,40,512]{3,2,1,0:T(8,128)(2,1)S(1)}, bf16[8,4,40,512]{3,2,1,0:T(8,128)(2,1)}, u32[]{:S(2)}) copy-start(bf16[8,4,40,512]{3,2,1,0:T(8,128)(2,1)} %param.6) | copy-start | bytes 3932164
  6.5 130.6 %copy-start.4 = (f32[512]{0:T(512)S(1)}, f32[512]{0:T(512)}, u32[]{:S(2)}) copy-start(f32[512]{0:T(512)} %param.7) | copy-start | bytes 6148
  6.5 130.6 %copy-start.3 = (f32[512]{0:T(512)S(1)}, f32[512]{0:T(512)}, u32[]{:S(2)}) copy-start(f32[512]{0:T(512)} %param.8) | copy-start | bytes 6148
  138.1 7.4 %collective-permute-start = (bf16[2,4,40,512]{3,2,1,0:T(8,128)(2,1)S(1)}, bf16[2,4,40,512]{3,2,1,0:T(8,128)(2,1)S(1)}, u32[]{:S(2)}, u32[]{:S(2)}) collective-permute-start(bf16[2,4,40,512]{3,2,1,0:T(8,128)(2,1)S(1)} %slice.133), channel_id=1, source_target_pairs={{0,4},{4,8},{8,12},{12,16},{16,20},{20,24},{24,28},{1,5},{5,9},{9,... | collective-permute-start | bytes 983048 | tf_op jit(solution)/shard_map/ppermute | solution.py:15
  170.1 24.9 %all-to-all-start = ((bf16[4,2,102400]{2,1,0:T(2,128)(2,1)}), bf16[4,2,102400]{2,1,0:T(2,128)(2,1)S(1)}, u32[]{:S(2)}, u32[]{:S(2)}) async-start(bf16[4,2,102400]{2,1,0:T(2,128)(2,1)} %reshape.28), calls=%async_computation | async-start | bytes 3276800 | tf_op jit(solution)/shard_map/all_to_all | solution.py:37
  173.7 300.8 %all-reduce.4.cloned.1.call-start = ((), (), s32[]{:S(2)}) async-start(), calls=%async_computation.1 | async-start | bytes 20971520
  253.5 3.0 copy-start.1
  281.5 0.7 copy-start.5
  281.5 193.0 %copy-start.2 = (bf16[8,4,40,512]{3,2,1,0:T(8,128)(2,1)S(1)}, bf16[8,4,40,512]{3,2,1,0:T(8,128)(2,1)}, u32[]{:S(2)}) copy-start(bf16[8,4,40,512]{3,2,1,0:T(8,128)(2,1)} %param.5) | copy-start | bytes 3932164
Sparse Core Ops, SparseCore 0:
  281.7 192.7 all-reduce.3
where the time goes:
time: 485 us
  waiting for transfers between devices  214 us (44%)
  blocking collectives  127 us (26%)
  local copies, waits for them, and re-layouts  90.5 us (19%)
  matrix products  25 us (5%)
  between operations  14.2 us (3%)
  other arithmetic  9.23 us (2%)
  starting transfers between devices  5.53 us (1%)
    unnamed x2, waiting for transfers between devices  191 us
    psum x1, blocking collectives, normalize(): mean = lax.psum(local_sum, ('frame', 'row')) / count  63.8 us
    psum x1, blocking collectives, normalize(): lax.psum(jnp.sum(centered * centered, axis=(0, 2)), ('frame', 'row'))  62.7 us
    unnamed x41, local copies, waits for them, and re-layouts  61.7 us
    dot_general x1, matrix products, convolve(): jnp.dot(columns, weight_part.reshape(-1, width), preferred_element_type=j...  25 us
    all_to_all x1, waiting for transfers between devices, convolve(): lax.all_to_all(lead, 'row', split_axis=3, concat_axis=1, tiled=True)  17.1 us
    concatenate x1, local copies, waits for them, and re-layouts, time_padded(): return jnp.concatenate([lead, act], axis=0)  12.8 us
  transfers between devices with their start and end apart: 3, of which 3 were waited for; matrix products, arithmetic and copies ran while one was open for 1% of the time, Pallas kernels for 0%

commit v1 on v0

v1 whole, which is shorter than its diff:
```python
import functools

import jax
import jax.numpy as jnp
from jax import lax
from jax.experimental import pallas as pl
from jax.experimental.pallas import tpu as pltpu
from jax.sharding import PartitionSpec as P

C = 512
MEMBERS = 16
FRAMES = 8
ROWS = 4
COLS = 40
OWN = ROWS * COLS
TALL = (ROWS + 2) * COLS
BLOCK = 2
VMEM = pl.BlockSpec(memory_space=pltpu.VMEM)


def stats_kernel(own, out):
    values = own[...].reshape(FRAMES * OWN, C).astype(jnp.float32)
    mean = jnp.sum(values, axis=0, keepdims=True) * (1.0 / (FRAMES * OWN))
    centered = own[...].reshape(FRAMES * OWN, C).astype(jnp.float32) - mean
    spread = jnp.sum(centered * centered, axis=0, keepdims=True)
    out[...] = jnp.concatenate([mean, spread], axis=0)


def local_stats(own):
    return pl.pallas_call(
        stats_kernel,
        out_shape=jax.ShapeDtypeStruct((2, C), jnp.float32),
        in_specs=[VMEM],
        out_specs=VMEM,
        compiler_params=pltpu.CompilerParams(vmem_limit_bytes=16 * 2**20),
    )(own)


def merge_stats(pairs):
    devices = pairs.shape[0]
    cells = FRAMES * OWN
    means = pairs[:, 0]
    mean = jnp.sum(means, axis=0, keepdims=True) * (1.0 / devices)
    off = means - mean
    spread = jnp.sum(pairs[:, 1] + off * off * float(cells), axis=0, keepdims=True)
    both = jnp.concatenate([mean, spread], axis=0)
    lane = lax.broadcasted_iota(jnp.int32, (2, C), 1)
    count = float(cells * devices)
    step = 1
    while step < MEMBERS:
        other = jnp.where((lane & step) != 0, pltpu.roll(both, step, 1), pltpu.roll(both, C - step, 1))
        gap = both[0:1] - other[0:1]
        mean = 0.5 * (both[0:1] + other[0:1])
        spread = both[1:2] + other[1:2] + gap * gap * (0.5 * count)
        both = jnp.concatenate([mean, spread], axis=0)
        count *= 2.0
        step *= 2
    return both[0:1], both[1:2] * (1.0 / count)


def conv_kernel(place, pairs, gain, bias, own, prev, up, down, up_prev, down_prev, latents, weight, out, tall, flat, held, sums, sems):
    def fetch(p, q):
        return pltpu.make_async_copy(weight.at[p, q], held.at[3 * p + q], sems.at[3 * p + q])

    for p in range(3):
        for q in range(3):
            fetch(p, q).start()

    mean, variance = merge_stats(pairs[...])
    scale = gain[...] / jnp.sqrt(variance + 1e-06)
    shift = bias[...]
    first = place[0] == 0
    keep_up = jnp.where(place[1] == 0, 0.0, 1.0)
    keep_down = jnp.where(place[1] == 3, 0.0, 1.0)

    def activate(values):
        normed = (values.astype(jnp.float32) - mean) * scale + shift
        half = 0.5 * normed
        return half + half * jnp.tanh(half)

    def frame(s):
        if s < 2:
            middle = jnp.where(first, own[0], prev[s])
            above = jnp.where(first, up[0], up_prev[s])
            below = jnp.where(first, down[0], down_prev[s])
        else:
            middle, above, below = own[s - 2], up[s - 2], down[s - 2]
        middle = activate(middle)
        above = activate(above) * keep_up
        below = activate(below) * keep_down
        flat[s] = middle.astype(jnp.bfloat16)
        tall[s] = jnp.concatenate([above, middle, below], axis=0).astype(jnp.bfloat16)

    def slab(s, q):
        if q == 1:
            part = flat[s : s + BLOCK]
        else:
            part = tall[s : s + BLOCK, q * COLS : q * COLS + OWN]
        return part.reshape(BLOCK * OWN, C)

    cells = BLOCK * OWN
    column = lax.rem(lax.broadcasted_iota(jnp.int32, (cells, 1), 0), COLS)
    for s in range(BLOCK + 2):
        frame(s)
    for t in range(0, FRAMES, BLOCK):
        for p in range(3):
            for q in range(3):
                if t == 0:
                    fetch(p, q).wait()
                part = slab(t + p, q)
                for r in range(3):
                    term = jnp.dot(part, held[3 * p + q, r], preferred_element_type=jnp.float32)
                    if p == 0 and q == 0:
                        sums[r] = term
                    else:
                        sums[r] += term
        left = jnp.where(column == 0, 0.0, pltpu.roll(sums[0], 1, 0))
        right = jnp.where(column == COLS - 1, 0.0, pltpu.roll(sums[2], cells - 1, 0))
        total = left + sums[1] + right + latents[t : t + BLOCK].reshape(cells, C).astype(jnp.float32)
        out[t : t + BLOCK] = total.astype(jnp.bfloat16).reshape(BLOCK, OWN, C)
        for s in range(t + BLOCK + 2, min(t + 2 * BLOCK + 2, FRAMES + 2)):
            frame(s)


def convolve(place, pairs, gain, bias, own, halos, latents, weight):
    return pl.pallas_call(
        conv_kernel,
        out_shape=jax.ShapeDtypeStruct((FRAMES, OWN, C), jnp.bfloat16),
        in_specs=[pl.BlockSpec(memory_space=pltpu.SMEM)] + [VMEM] * 10 + [pl.BlockSpec(memory_space=pl.ANY)],
        out_specs=VMEM,
        scratch_shapes=[
            pltpu.VMEM((FRAMES + 2, TALL, C), jnp.bfloat16),
            pltpu.VMEM((FRAMES + 2, OWN, C), jnp.bfloat16),
            pltpu.VMEM((9, 3, C, C), jnp.bfloat16),
            pltpu.VMEM((3, BLOCK * OWN, C), jnp.float32),
            pltpu.SemaphoreType.DMA((9,)),
        ],
        compiler_params=pltpu.CompilerParams(vmem_limit_bytes=56 * 2**20),
    )(place, pairs, gain, bias, own, *halos, latents, weight)


def send(block, by_frame, by_row):
    frames, rows = lax.axis_size("frame"), lax.axis_size("row")
    pairs = []
    for f in range(frames):
        for r in range(rows):
            g, s = f + by_frame, r + by_row
            if 0 <= g < frames and 0 <= s < rows:
                pairs.append((f * rows + r, g * rows + s))
    return lax.ppermute(block, ("frame", "row"), pairs)


def shards(latents, hidden, norm_gain, norm_bias, conv_weight):
    own = hidden.reshape(FRAMES, OWN, C)
    last_row, first_row = own[:, OWN - COLS :], own[:, :COLS]
    up = send(last_row, 0, 1)
    down = send(first_row, 0, -1)
    prev = send(own[-2:], 1, 0)
    up_prev = send(last_row[-2:], 1, 1)
    down_prev = send(first_row[-2:], 1, -1)
    stats = local_stats(own)
    members = lax.axis_size("frame") * lax.axis_size("row")
    copies = jnp.broadcast_to(stats[None], (members, 2, C))
    pairs = lax.all_to_all(copies, ("frame", "row"), 0, 0, tiled=True)
    place = jnp.stack([lax.axis_index("frame"), lax.axis_index("row")]).astype(jnp.int32)
    result = convolve(
        place,
        pairs,
        norm_gain.reshape(1, C),
        norm_bias.reshape(1, C),
        own,
        (prev, up, down, up_prev, down_prev),
        latents.reshape(FRAMES, OWN, C),
        conv_weight,
    )
    return result.reshape(FRAMES, ROWS, COLS, C)


def solution(mesh):
    in_specs = (
        P(("clip", "frame"), "row", None, None),
        P(("clip", "frame"), "row", None, None),
        P(),
        P(),
        P(),
    )
    out_specs = P(("clip", "frame"), "row", None, None)
    return jax.shard_map(shards, mesh=mesh, in_specs=in_specs, out_specs=out_specs, check_vma=False)
```

time: 485 us -> 54.4 us (0.11)
  waiting for transfers between devices: 214 us -> 0.89 us
  blocking collectives: 127 us -> 0 us
  local copies, waits for them, and re-layouts: 90.5 us -> 3.71 us
  matrix products: 25 us -> 0 us
  Pallas kernels: 0 us -> 24.5 us
  starting transfers between devices: 5.53 us -> 23.9 us
  between operations: 14.2 us -> 0.14 us
  other arithmetic: 9.23 us -> 0.58 us
    unnamed x2 -> x0, waiting for transfers between devices: 191 us -> none
    psum x2 -> x0, blocking collectives: 127 us -> none  [the longest x1 63.8 us: normalize(): mean = lax.psum(local_sum, ('frame', 'row')) / count]
    unnamed x41 -> x16, local copies, waits for them, and re-layouts: 61.7 us -> 2.29 us
    dot_general x1 -> x0, matrix products: 25 us -> none  [convolve(): jnp.dot(columns, weight_part.reshape(-1, width), preferred_element_type=j...]
    pallas_call x0 -> x2, Pallas kernels: none -> 24.5 us  [the longest x1 23.8 us: convolve(): pl.pallas_call(conv_kernel, out_shape=jax.ShapeDtypeStruct((FRAMES, OWN,...]
    all_to_all x1, waiting for transfers between devices: 17.1 us -> 0.01 us  [shards(): pairs = lax.all_to_all(copies, ('frame', 'row'), 0, 0, tiled=True)]
    concatenate x2 -> x0, local copies, waits for them, and re-layouts: 14.5 us -> none  [the longest x1 12.8 us: time_padded(): return jnp.concatenate([lead, act], axis=0)]
    ppermute x1 -> x5, starting transfers between devices: 1.92 us -> 15.3 us  [send(): return lax.ppermute(block, ('frame', 'row'), pairs)]
  transfers between devices with their start and end apart: 3 -> 6, of which waited for: 3 -> 1; matrix products, arithmetic and copies ran while one was open for 1% -> 2% of each run, Pallas kernels for 0% -> 0%
where the time goes in v1:
time: 54.4 us; the launch traced here: 53.7 us
  Pallas kernels  24.5 us (45%)
  starting transfers between devices  23.9 us (44%)
  local copies, waits for them, and re-layouts  3.71 us (7%)
  waiting for transfers between devices  0.89 us (2%)
  other arithmetic  0.58 us (1%)
    pallas_call x1, Pallas kernels, convolve(): pl.pallas_call(conv_kernel, out_shape=jax.ShapeDtypeStruct((FRAMES, OWN,...  23.8 us
    ppermute x5, starting transfers between devices, send(): return lax.ppermute(block, ('frame', 'row'), pairs)  15.3 us
    all_to_all x1, starting transfers between devices, shards(): pairs = lax.all_to_all(copies, ('frame', 'row'), 0, 0, tiled=True)  8.59 us
    unnamed x16, local copies, waits for them, and re-layouts  2.29 us
  transfers between devices with their start and end apart: 6, of which 1 were waited for; matrix products, arithmetic and copies ran while one was open for 2% of the time, Pallas kernels for 0%

profile of v1, /device:TPU:1, one launch (start us, length us, event | category | flops | bytes accessed | tf_op | source)
XLA Modules:
  0.0 53.7 jit_solution(2643423940217737107)
XLA Ops:
  0.0 1.3 %copy-done = bf16[8,4,40,512]{3,2,1,0:T(8,128)(2,1)S(1)} copy-done((bf16[8,4,40,512]{3,2,1,0:T(8,128)(2,1)S(1)}, bf16[8,4,40,512]{3,2,1,0:T(8,128)(2,1)}, u32[]{:S(2)}) %copy-start) | copy-done | bytes 1310744
  1.3 0.7 %shard_map.55 = f32[2,512]{1,0:T(2,128)S(1)} custom-call(bf16[8,160,512]{2,1,0:T(8,128)(2,1)S(1)} %bitcast.9), custom_call_target="tpu_custom_call" | custom-call | tf_op jit(solution)/shard_map/pallas_call | solution.py:30
  2.0 0.7 %broadcast_in_dim.2 = f32[32,2,512]{2,1,0:T(2,128)} broadcast(f32[2,512]{1,0:T(2,128)S(1)} %shard_map.55), dimensions={1,2} | broadcast | bytes 135168 | tf_op jit(solution)/shard_map/broadcast_in_dim | solution.py:163
  2.7 8.6 %all-to-all-start = ((f32[32,2,512]{2,1,0:T(2,128)}), f32[32,2,512]{2,1,0:T(2,128)S(1)}, u32[]{:S(2)}, u32[]{:S(2)}) async-start(f32[32,2,512]{2,1,0:T(2,128)} %broadcast_in_dim.2), calls=%async_computation | async-start | bytes 262144 | tf_op jit(solution)/shard_map/all_to_all | solution.py:164
  11.3 3.5 %collective-permute-start = (bf16[2,160,512]{2,1,0:T(8,128)(2,1)S(1)}, bf16[2,160,512]{2,1,0:T(8,128)(2,1)S(1)}, u32[]{:S(2)}, u32[]{:S(2)}) collective-permute-start(bf16[2,160,512]{2,1,0:T(8,128)(2,1)S(1)} %bitcast.13), channel_id=1, source_target_pairs={{0,4},{1,5},{2,6},{3,7},{4,8},{5,9},{6,10},{7,11},{8,12},{9,13},{1... | collective-permute-start | bytes 983048 | tf_op jit(solution)/shard_map/ppermute | solution.py:150
  14.9 0.1 fusion.1
  14.9 1.3 %collective-permute-start.2 = (bf16[8,40,512]{2,1,0:T(8,128)(2,1)S(1)}, bf16[8,40,512]{2,1,0:T(8,128)(2,1)S(1)}, u32[]{:S(2)}, u32[]{:S(2)}) collective-permute-start(bf16[8,40,512]{2,1,0:T(8,128)(2,1)S(1)} %get-tuple-element.7), channel_id=1, source_target_pairs={{1,0},{2,1},{3,2},{5,4},{6,5},{7,6},{9,8},{10,9},{11,10},{13,12},{... | collective-permute-start | bytes 983048 | tf_op jit(solution)/shard_map/ppermute | solution.py:150
  16.2 4.0 %collective-permute-start.1 = (bf16[8,40,512]{2,1,0:T(8,128)(2,1)S(1)}, bf16[8,40,512]{2,1,0:T(8,128)(2,1)S(1)}, u32[]{:S(2)}, u32[]{:S(2)}) collective-permute-start(bf16[8,40,512]{2,1,0:T(8,128)(2,1)S(1)} %get-tuple-element.8), channel_id=1, source_target_pairs={{0,1},{1,2},{2,3},{4,5},{5,6},{6,7},{8,9},{9,10},{10,11},{12,13},{... | collective-permute-start | bytes 983048 | tf_op jit(solution)/shard_map/ppermute | solution.py:150
  20.3 0.7 %fusion = (bf16[2,40,512]{2,1,0:T(8,128)(2,1)}, bf16[2,40,512]{2,1,0:T(8,128)(2,1)S(1)}) fusion(bf16[8,160,512]{2,1,0:T(8,128)(2,1)S(1)} %bitcast.11), kind=kLoop, calls=%fused_computation.1 | loop fusion | bytes 327680 | tf_op jit(solution)/shard_map/slice | solution.py:160
  20.9 1.3 %collective-permute-start.4 = (bf16[2,40,512]{2,1,0:T(8,128)(2,1)}, bf16[2,40,512]{2,1,0:T(8,128)(2,1)S(1)}, u32[]{:S(2)}, u32[]{:S(2)}) collective-permute-start(bf16[2,40,512]{2,1,0:T(8,128)(2,1)} %get-tuple-element.5), channel_id=1, source_target_pairs={{1,4},{2,5},{3,6},{5,8},{6,9},{7,10},{9,12},{10,13},{11,14},{13,16... | collective-permute-start | bytes 245768 | tf_op jit(solution)/shard_map/ppermute | solution.py:150
  22.2 5.2 %collective-permute-start.3 = (bf16[2,40,512]{2,1,0:T(8,128)(2,1)S(1)}, bf16[2,40,512]{2,1,0:T(8,128)(2,1)S(1)}, u32[]{:S(2)}, u32[]{:S(2)}) collective-permute-start(bf16[2,40,512]{2,1,0:T(8,128)(2,1)S(1)} %get-tuple-element.6), channel_id=1, source_target_pairs={{0,5},{1,6},{2,7},{4,9},{5,10},{6,11},{8,13},{9,14},{10,15},{12,17... | collective-permute-start | bytes 245768 | tf_op jit(solution)/shard_map/ppermute | solution.py:150
  27.4 0.6 %pad_add_fusion.place = s32[2]{0:T(128)} fusion(s32[1]{0:T(128)} %bitcast.1, s32[1]{0:T(128)} %bitcast), kind=kLoop, calls=%fused_computation | loop fusion | flops 2 | bytes 16 | tf_op jit(solution)/shard_map/stack | solution.py:165
  28.0 0.0 collective-permute-done.4.down_prev
  28.0 0.9 %collective-permute-done.3.up_prev = bf16[2,40,512]{2,1,0:T(8,128)(2,1)S(1)} collective-permute-done((bf16[2,40,512]{2,1,0:T(8,128)(2,1)S(1)}, bf16[2,40,512]{2,1,0:T(8,128)(2,1)S(1)}, u32[]{:S(2)}, u32[]{:S(2)}) %collective-permute-start.3) | collective-permute-done | bytes 81952 | tf_op jit(solution)/shard_map/ppermute | solution.py:150
  28.8 0.0 all-to-all-done.pairs
  28.8 0.0 collective-permute-done.prev
  28.9 0.0 collective-permute-done.2.down
  28.9 0.0 collective-permute-done.1.up
  28.9 0.6 %copy-done.7 = bf16[2,40,512]{2,1,0:T(8,128)(2,1)} copy-done((bf16[2,40,512]{2,1,0:T(8,128)(2,1)}, bf16[2,40,512]{2,1,0:T(8,128)(2,1)S(1)}, u32[]{:S(2)}) %copy-start.7) | copy-done | bytes 81944
  29.5 0.1 copy-done.2
  29.5 0.1 copy-done.3
  29.7 0.1 copy-done.4
  29.7 0.1 copy-done.5
  29.9 23.8 %shard_map.56 = bf16[8,160,512]{2,1,0:T(8,128)(2,1)} custom-call(s32[2]{0:T(128)} %pad_add_fusion.place, f32[32,2,512]{2,1,0:T(2,128)} %copy-done.2, f32[1,512]{1,0:T(1,128)} %bitcast.14, f32[1,512]{1,0:T(1,128)} %bitcast.15, bf16[8,160,512]{2,1,0:T(8,128)(2,1)} %bitcast.8, bf16[2,160,512]{2,1,0:T(8,128)(2,1)} %copy-done.3, bf16[8,40,512]{2,1,0:T(8,128)(2,1)} %copy-done.5, ...), custom_call_target="tpu_custom_call" | custom-call | tf_op jit(solution)/shard_map/pallas_call | solution.py:126
  (11 shorter events, 0.0 us)
Async XLA Ops:
  0.0 1.3 %copy-start = (bf16[8,4,40,512]{3,2,1,0:T(8,128)(2,1)S(1)}, bf16[8,4,40,512]{3,2,1,0:T(8,128)(2,1)}, u32[]{:S(2)}) copy-start(bf16[8,4,40,512]{3,2,1,0:T(8,128)(2,1)} %param.6) | copy-start | bytes 3932164
  1.3 10.0 %copy-start.1 = (bf16[8,4,40,512]{3,2,1,0:T(8,128)(2,1)S(1)}, bf16[8,4,40,512]{3,2,1,0:T(8,128)(2,1)}, u32[]{:S(2)}) copy-start(bf16[8,4,40,512]{3,2,1,0:T(8,128)(2,1)} %param.6) | copy-start | bytes 3932164
  2.7 26.2 %all-to-all-start = ((f32[32,2,512]{2,1,0:T(2,128)}), f32[32,2,512]{2,1,0:T(2,128)S(1)}, u32[]{:S(2)}, u32[]{:S(2)}) async-start(f32[32,2,512]{2,1,0:T(2,128)} %broadcast_in_dim.2), calls=%async_computation | async-start | bytes 262144 | tf_op jit(solution)/shard_map/all_to_all | solution.py:164
  11.3 17.5 %collective-permute-start = (bf16[2,160,512]{2,1,0:T(8,128)(2,1)S(1)}, bf16[2,160,512]{2,1,0:T(8,128)(2,1)S(1)}, u32[]{:S(2)}, u32[]{:S(2)}) collective-permute-start(bf16[2,160,512]{2,1,0:T(8,128)(2,1)S(1)} %bitcast.13), channel_id=1, source_target_pairs={{0,4},{1,5},{2,6},{3,7},{4,8},{5,9},{6,10},{7,11},{8,12},{9,13},{1... | collective-permute-start | bytes 983048 | tf_op jit(solution)/shard_map/ppermute | solution.py:150
  14.9 13.9 %collective-permute-start.2 = (bf16[8,40,512]{2,1,0:T(8,128)(2,1)S(1)}, bf16[8,40,512]{2,1,0:T(8,128)(2,1)S(1)}, u32[]{:S(2)}, u32[]{:S(2)}) collective-permute-start(bf16[8,40,512]{2,1,0:T(8,128)(2,1)S(1)} %get-tuple-element.7), channel_id=1, source_target_pairs={{1,0},{2,1},{3,2},{5,4},{6,5},{7,6},{9,8},{10,9},{11,10},{13,12},{... | collective-permute-start | bytes 983048 | tf_op jit(solution)/shard_map/ppermute | solution.py:150
  16.2 12.6 %collective-permute-start.1 = (bf16[8,40,512]{2,1,0:T(8,128)(2,1)S(1)}, bf16[8,40,512]{2,1,0:T(8,128)(2,1)S(1)}, u32[]{:S(2)}, u32[]{:S(2)}) collective-permute-start(bf16[8,40,512]{2,1,0:T(8,128)(2,1)S(1)} %get-tuple-element.8), channel_id=1, source_target_pairs={{0,1},{1,2},{2,3},{4,5},{5,6},{6,7},{8,9},{9,10},{10,11},{12,13},{... | collective-permute-start | bytes 983048 | tf_op jit(solution)/shard_map/ppermute | solution.py:150
  20.9 7.1 %collective-permute-start.4 = (bf16[2,40,512]{2,1,0:T(8,128)(2,1)}, bf16[2,40,512]{2,1,0:T(8,128)(2,1)S(1)}, u32[]{:S(2)}, u32[]{:S(2)}) collective-permute-start(bf16[2,40,512]{2,1,0:T(8,128)(2,1)} %get-tuple-element.5), channel_id=1, source_target_pairs={{1,4},{2,5},{3,6},{5,8},{6,9},{7,10},{9,12},{10,13},{11,14},{13,16... | collective-permute-start | bytes 245768 | tf_op jit(solution)/shard_map/ppermute | solution.py:150
  22.2 6.6 %collective-permute-start.3 = (bf16[2,40,512]{2,1,0:T(8,128)(2,1)S(1)}, bf16[2,40,512]{2,1,0:T(8,128)(2,1)S(1)}, u32[]{:S(2)}, u32[]{:S(2)}) collective-permute-start(bf16[2,40,512]{2,1,0:T(8,128)(2,1)S(1)} %get-tuple-element.6), channel_id=1, source_target_pairs={{0,5},{1,6},{2,7},{4,9},{5,10},{6,11},{8,13},{9,14},{10,15},{12,17... | collective-permute-start | bytes 245768 | tf_op jit(solution)/shard_map/ppermute | solution.py:150
  28.0 0.9 %copy-start.6 = (bf16[2,40,512]{2,1,0:T(8,128)(2,1)}, bf16[2,40,512]{2,1,0:T(8,128)(2,1)S(1)}, u32[]{:S(2)}) copy-start(bf16[2,40,512]{2,1,0:T(8,128)(2,1)S(1)} %collective-permute-done.4.down_prev) | copy-start | bytes 245764
  28.8 0.6 %copy-start.7 = (bf16[2,40,512]{2,1,0:T(8,128)(2,1)}, bf16[2,40,512]{2,1,0:T(8,128)(2,1)S(1)}, u32[]{:S(2)}) copy-start(bf16[2,40,512]{2,1,0:T(8,128)(2,1)S(1)} %collective-permute-done.3.up_prev) | copy-start | bytes 245764
  28.8 0.7 %copy-start.2 = (f32[32,2,512]{2,1,0:T(2,128)}, f32[32,2,512]{2,1,0:T(2,128)S(1)}, u32[]{:S(2)}) copy-start(f32[32,2,512]{2,1,0:T(2,128)S(1)} %all-to-all-done.pairs) | copy-start | bytes 393220
  28.9 0.8 %copy-start.3 = (bf16[2,160,512]{2,1,0:T(8,128)(2,1)}, bf16[2,160,512]{2,1,0:T(8,128)(2,1)S(1)}, u32[]{:S(2)}) copy-start(bf16[2,160,512]{2,1,0:T(8,128)(2,1)S(1)} %collective-permute-done.prev) | copy-start | bytes 983044
  28.9 0.9 %copy-start.4 = (bf16[8,40,512]{2,1,0:T(8,128)(2,1)}, bf16[8,40,512]{2,1,0:T(8,128)(2,1)S(1)}, u32[]{:S(2)}) copy-start(bf16[8,40,512]{2,1,0:T(8,128)(2,1)S(1)} %collective-permute-done.2.down) | copy-start | bytes 983044
  28.9 1.0 %copy-start.5 = (bf16[8,40,512]{2,1,0:T(8,128)(2,1)}, bf16[8,40,512]{2,1,0:T(8,128)(2,1)S(1)}, u32[]{:S(2)}) copy-start(bf16[8,40,512]{2,1,0:T(8,128)(2,1)S(1)} %collective-permute-done.1.up) | copy-start | bytes 983044

commit v2 on v1

v2 whole, which is shorter than its diff:
```python
import functools

import jax
import jax.numpy as jnp
from jax import lax
from jax.experimental import pallas as pl
from jax.experimental.pallas import tpu as pltpu
from jax.sharding import PartitionSpec as P

C = 512
MEMBERS = 16
FRAMES = 8
ROWS = 4
COLS = 40
OWN = ROWS * COLS
INNER = 2 * COLS
BLOCK = 4
ROW_SHARDS = 4
WINDOW = 3
TAPS = 9
VMEM = pl.BlockSpec(memory_space=pltpu.VMEM)


HBM = pl.BlockSpec(memory_space=pltpu.HBM)
SMALL = pl.BlockSpec(memory_space=pltpu.SMEM)
WINDOWED = FRAMES + 2


def bf16(*shape):
    return jax.ShapeDtypeStruct(shape, jnp.bfloat16)


def stats_kernel(own, out, tail):
    values = own[...].reshape(FRAMES * OWN, C).astype(jnp.float32)
    mean = jnp.sum(values, axis=0, keepdims=True) * (1.0 / (FRAMES * OWN))
    centered = own[...].reshape(FRAMES * OWN, C).astype(jnp.float32) - mean
    spread = jnp.sum(centered * centered, axis=0, keepdims=True)
    both = jnp.concatenate([mean, spread], axis=0)
    out[...] = jnp.broadcast_to(both[None], out.shape)
    tail[...] = own[FRAMES - 2 :]


def local_stats(own, copies):
    return pl.pallas_call(
        stats_kernel,
        out_shape=(jax.ShapeDtypeStruct((copies, 2, C), jnp.float32), bf16(2, OWN, C)),
        in_specs=[VMEM],
        out_specs=(VMEM, VMEM),
        compiler_params=pltpu.CompilerParams(vmem_limit_bytes=8 * 2**20),
        cost_estimate=pl.CostEstimate(flops=4 * 10**9, bytes_accessed=100 * 2**20, transcendentals=0),
    )(own)


def merge_stats(pairs):
    devices = pairs.shape[0]
    cells = FRAMES * OWN
    means = pairs[:, 0]
    mean = jnp.sum(means, axis=0, keepdims=True) * (1.0 / devices)
    off = means - mean
    spread = jnp.sum(pairs[:, 1] + off * off * float(cells), axis=0, keepdims=True)
    both = jnp.concatenate([mean, spread], axis=0)
    lane = lax.broadcasted_iota(jnp.int32, (2, C), 1)
    count = float(cells * devices)
    step = 1
    while step < MEMBERS:
        other = jnp.where((lane & step) != 0, pltpu.roll(both, step, 1), pltpu.roll(both, C - step, 1))
        gap = both[0:1] - other[0:1]
        mean = 0.5 * (both[0:1] + other[0:1])
        spread = both[1:2] + other[1:2] + gap * gap * (0.5 * count)
        both = jnp.concatenate([mean, spread], axis=0)
        count *= 2.0
        step *= 2
    return both[0:1], both[1:2] * (1.0 / count)


def border_kernel(own, prev, bottom, top):
    bottom[:2] = prev[:, 3 * COLS :]
    bottom[2:] = own[:, 3 * COLS :]
    top[:2] = prev[:, :COLS]
    top[2:] = own[:, :COLS]


def border_rows(own, prev):
    shape = bf16(WINDOWED, COLS, C)
    return pl.pallas_call(
        border_kernel,
        out_shape=(shape, shape),
        in_specs=[VMEM, VMEM],
        out_specs=(VMEM, VMEM),
        compiler_params=pltpu.CompilerParams(vmem_limit_bytes=8 * 2**20),
        cost_estimate=pl.CostEstimate(flops=10**10, bytes_accessed=200 * 2**20, transcendentals=0),
    )(own, prev)


def activate(values, mean, scale, shift):
    normed = (values.astype(jnp.float32) - mean) * scale + shift
    half = 0.5 * normed
    return half + half * jnp.tanh(half)


def accumulate(sums, taps, slab, frame, finish):
    cells = BLOCK * INNER
    column = lax.rem(lax.broadcasted_iota(jnp.int32, (cells, 1), 0), COLS)
    for s in range(BLOCK + 2):
        frame(s)
    for t in range(0, FRAMES, BLOCK):
        for p in range(3):
            for q in range(3):
                held = taps(3 * p + q, t == 0)
                part = slab(t + p, q).reshape(cells, C)
                for r in range(3):
                    term = jnp.dot(part, held[r], preferred_element_type=jnp.float32)
                    if p == 0 and q == 0:
                        sums[r] = term
                    else:
                        sums[r] += term
        left = jnp.where(column == 0, 0.0, pltpu.roll(sums[0], 1, 0))
        right = jnp.where(column == COLS - 1, 0.0, pltpu.roll(sums[2], cells - 1, 0))
        finish(t, (left + sums[1] + right).reshape(BLOCK, INNER, C))
        for s in range(t + BLOCK + 2, min(t + 2 * BLOCK + 2, WINDOWED)):
            frame(s)


def inner_kernel(place, pairs, gain, bias, own, prev, latents, weight, out, middle, ends, coef, held, tall, sums, sems):
    copies = [
        pltpu.make_async_copy(weight.at[i // 3, i % 3], held.at[i], sems.at[i])
        for i in range(TAPS)
    ]
    for copy in copies[:WINDOW]:
        copy.start()
    mean, variance = merge_stats(pairs[...])
    scale = gain[...] / jnp.sqrt(variance + 1e-06)
    shift = bias[...]
    coef[...] = jnp.concatenate([mean, scale, shift], axis=0)
    first = place[0] == 0

    def taps(i, once):
        if once:
            copies[i].wait()
            if i + WINDOW < TAPS:
                copies[i + WINDOW].start()
        return held.at[i]

    def frame(s):
        values = jnp.where(first, own[0], prev[s]) if s < 2 else own[s - 2]
        values = activate(values, mean, scale, shift)
        tall[s] = values.astype(jnp.bfloat16)
        middle[s] = values[COLS : 3 * COLS].astype(jnp.bfloat16)
        ends[s] = jnp.concatenate([values[:COLS], values[3 * COLS :]], axis=0).astype(jnp.bfloat16)

    def slab(s, q):
        if q == 1:
            return middle[s : s + BLOCK]
        return tall[s : s + BLOCK, q * COLS : q * COLS + INNER]

    def finish(t, total):
        skip = latents[t : t + BLOCK].astype(jnp.float32)[:, COLS : 3 * COLS]
        out[t : t + BLOCK] = (total + skip).astype(jnp.bfloat16)

    accumulate(sums, taps, slab, frame, finish)


def inner_call(place, pairs, gain, bias, own, prev, latents, weight):
    return pl.pallas_call(
        inner_kernel,
        out_shape=(
            bf16(FRAMES, INNER, C),
            bf16(WINDOWED, INNER, C),
            bf16(WINDOWED, INNER, C),
            jax.ShapeDtypeStruct((3, C), jnp.float32),
            bf16(TAPS, 3, C, C),
        ),
        in_specs=[SMALL] + [VMEM] * 6 + [HBM],
        out_specs=(VMEM,) * 5,
        scratch_shapes=[
            pltpu.VMEM((WINDOWED, OWN, C), jnp.bfloat16),
            pltpu.VMEM((3, BLOCK * INNER, C), jnp.float32),
            pltpu.SemaphoreType.DMA((TAPS,)),
        ],
        compiler_params=pltpu.CompilerParams(vmem_limit_bytes=28 * 2**20),
        cost_estimate=pl.CostEstimate(
            flops=FRAMES * INNER * 27 * C * C * 2, bytes_accessed=20 * 2**20, transcendentals=0
        ),
    )(place, pairs, gain, bias, own, prev, latents, weight)


def outer_kernel(place, coef, up, down, latents, inner, middle, ends, held, out, above_two, below_two, sums):
    mean, scale, shift = coef[0:1], coef[1:2], coef[2:3]
    first = place[0] == 0
    keep_up = jnp.where(place[1] == 0, 0.0, 1.0)
    keep_down = jnp.where(place[1] == ROW_SHARDS - 1, 0.0, 1.0)

    def taps(i, once):
        return held.at[i]

    def frame(s):
        above, below = up[s], down[s]
        if s < 2:
            above, below = jnp.where(first, up[2], above), jnp.where(first, down[2], below)
        above = activate(above, mean, scale, shift) * keep_up
        below = activate(below, mean, scale, shift) * keep_down
        between = middle[s].astype(jnp.float32)
        above_two[s] = jnp.concatenate([above, between[COLS:]], axis=0).astype(jnp.bfloat16)
        below_two[s] = jnp.concatenate([between[:COLS], below], axis=0).astype(jnp.bfloat16)

    def slab(s, q):
        return (above_two, ends, below_two)[q][s : s + BLOCK]

    def finish(t, total):
        skip = latents[t : t + BLOCK].astype(jnp.float32)
        top = total[:, :COLS] + skip[:, :COLS]
        bottom = total[:, COLS:] + skip[:, 3 * COLS :]
        between = inner[t : t + BLOCK].astype(jnp.float32)
        out[t : t + BLOCK] = jnp.concatenate([top, between, bottom], axis=1).astype(jnp.bfloat16)

    accumulate(sums, taps, slab, frame, finish)


def outer_call(*operands):
    return pl.pallas_call(
        outer_kernel,
        out_shape=bf16(FRAMES, OWN, C),
        in_specs=[SMALL] + [VMEM] * 8,
        out_specs=VMEM,
        scratch_shapes=[
            pltpu.VMEM((WINDOWED, INNER, C), jnp.bfloat16),
            pltpu.VMEM((WINDOWED, INNER, C), jnp.bfloat16),
            pltpu.VMEM((3, BLOCK * INNER, C), jnp.float32),
        ],
        compiler_params=pltpu.CompilerParams(vmem_limit_bytes=26 * 2**20),
        cost_estimate=pl.CostEstimate(
            flops=FRAMES * INNER * 27 * C * C * 2, bytes_accessed=20 * 2**20, transcendentals=0
        ),
    )(*operands)


def send(block, by_frame, by_row):
    frames, rows = lax.axis_size("frame"), lax.axis_size("row")
    pairs = []
    for f in range(frames):
        for r in range(rows):
            g, s = f + by_frame, r + by_row
            if 0 <= g < frames and 0 <= s < rows:
                pairs.append((f * rows + r, g * rows + s))
    return lax.ppermute(block, ("frame", "row"), pairs)


def shards(latents, hidden, norm_gain, norm_bias, conv_weight):
    own = hidden.reshape(FRAMES, OWN, C)
    skip = latents.reshape(FRAMES, OWN, C)
    members = lax.axis_size("frame") * lax.axis_size("row")
    copies, last_two = local_stats(own, members)
    prev = send(last_two, 1, 0)
    pairs = lax.all_to_all(copies, ("frame", "row"), 0, 0, tiled=True)
    bottom, top = border_rows(own, prev)
    up = send(bottom, 0, 1)
    down = send(top, 0, -1)
    place = jnp.stack([lax.axis_index("frame"), lax.axis_index("row")]).astype(jnp.int32)
    gain, bias = norm_gain.reshape(1, C), norm_bias.reshape(1, C)
    inner, middle, ends, coef, held = inner_call(place, pairs, gain, bias, own, prev, skip, conv_weight)
    result = outer_call(place, coef, up, down, skip, inner, middle, ends, held)
    return result.reshape(FRAMES, ROWS, COLS, C)


def solution(mesh):
    in_specs = (
        P(("clip", "frame"), "row", None, None),
        P(("clip", "frame"), "row", None, None),
        P(),
        P(),
        P(),
    )
    out_specs = P(("clip", "frame"), "row", None, None)
    return jax.shard_map(shards, mesh=mesh, in_specs=in_specs, out_specs=out_specs, check_vma=False)
```

time: 54.4 us -> 45.6 us (0.84)
  starting transfers between devices: 23.9 us -> 16 us
  local copies, waits for them, and re-layouts: 3.71 us -> 1.33 us
  Pallas kernels: 24.5 us -> 25.9 us
  waiting for transfers between devices: 0.89 us -> 1.93 us
    ppermute x5 -> x3, starting transfers between devices: 15.3 us -> 9.09 us  [send(): return lax.ppermute(block, ('frame', 'row'), pairs)]
    all_to_all x1, waiting for transfers between devices: 0.01 us -> 1.92 us  [shards(): pairs = lax.all_to_all(copies, ('frame', 'row'), 0, 0, tiled=True)]
    all_to_all x1, starting transfers between devices: 8.59 us -> 6.92 us  [shards(): pairs = lax.all_to_all(copies, ('frame', 'row'), 0, 0, tiled=True)]
    pallas_call x2 -> x4, Pallas kernels: 24.5 us -> 25.9 us  [the longest x1 12 us: inner_call(): pl.pallas_call(inner_kernel, out_shape=(bf16(FRAMES, INNER, C), bf16(WIND...]
    unnamed x16 -> x10, local copies, waits for them, and re-layouts: 2.29 us -> 1.33 us
    ppermute x5 -> x3, waiting for transfers between devices: 0.89 us -> 0.01 us  [send(): return lax.ppermute(block, ('frame', 'row'), pairs)]
    slice x3 -> x0, local copies, waits for them, and re-layouts: 0.73 us -> none  [the longest x1 0.65 us: shards(): down_prev = send(first_row[-2:], 1, -1)]
    broadcast_in_dim x1 -> x0, local copies, waits for them, and re-layouts: 0.69 us -> none  [shards(): copies = jnp.broadcast_to(stats[None], (members, 2, C))]
  transfers between devices with their start and end apart: 6 -> 4, of which waited for: 1 -> 1; matrix products, arithmetic and copies ran while one was open for 2% -> 0% of each run, Pallas kernels for 0% -> 29%
where the time goes in v2:
time: 45.6 us; the launch traced here: 45.3 us
  Pallas kernels  25.9 us (57%)
  starting transfers between devices  16 us (35%)
  waiting for transfers between devices  1.93 us (4%)
  local copies, waits for them, and re-layouts  1.33 us (3%)
    pallas_call x1, Pallas kernels, inner_call(): pl.pallas_call(inner_kernel, out_shape=(bf16(FRAMES, INNER, C), bf16(WIND...  12 us
    pallas_call x1, Pallas kernels, outer_call(): pl.pallas_call(outer_kernel, out_shape=bf16(FRAMES, OWN, C), in_specs=[SM...  11.6 us
    ppermute x3, starting transfers between devices, send(): return lax.ppermute(block, ('frame', 'row'), pairs)  9.09 us
    all_to_all x1, starting transfers between devices, shards(): pairs = lax.all_to_all(copies, ('frame', 'row'), 0, 0, tiled=True)  6.92 us
    all_to_all x1, waiting for transfers between devices, shards(): pairs = lax.all_to_all(copies, ('frame', 'row'), 0, 0, tiled=True)  1.92 us
    pallas_call x1, Pallas kernels, local_stats(): pl.pallas_call(stats_kernel, out_shape=(jax.ShapeDtypeStruct((copies, 2,...  1.34 us
    unnamed x10, local copies, waits for them, and re-layouts  1.33 us
    pallas_call x1, Pallas kernels, border_rows(): pl.pallas_call(border_kernel, out_shape=(shape, shape), in_specs=[VMEM, V...  0.94 us
  transfers between devices with their start and end apart: 4, of which 1 were waited for; matrix products, arithmetic and copies ran while one was open for 0% of the time, Pallas kernels for 29%

profile of v2, /device:TPU:1, one launch (start us, length us, event | category | flops | bytes accessed | tf_op | source)
XLA Modules:
  0.0 45.3 jit_solution(14697555844321306449)
XLA Ops:
  0.0 0.0 copy-start
  0.0 1.3 %copy-done = bf16[8,4,40,512]{3,2,1,0:T(8,128)(2,1)S(1)} copy-done((bf16[8,4,40,512]{3,2,1,0:T(8,128)(2,1)S(1)}, bf16[8,4,40,512]{3,2,1,0:T(8,128)(2,1)}, u32[]{:S(2)}) %copy-start) | copy-done | bytes 1310744
  1.3 0.0 copy-start.1
  1.3 1.3 %shard_map.55 = (f32[32,2,512]{2,1,0:T(2,128)}, bf16[2,160,512]{2,1,0:T(8,128)(2,1)S(1)}) custom-call(bf16[8,160,512]{2,1,0:T(8,128)(2,1)S(1)} %bitcast.7), custom_call_target="tpu_custom_call" | custom-call | flops 4000000000 | bytes 104857600 | tf_op jit(solution)/shard_map/pallas_call | solution.py:44
  2.7 4.5 %collective-permute-start = (bf16[2,160,512]{2,1,0:T(8,128)(2,1)S(1)}, bf16[2,160,512]{2,1,0:T(8,128)(2,1)S(1)}, u32[]{:S(2)}, u32[]{:S(2)}) collective-permute-start(bf16[2,160,512]{2,1,0:T(8,128)(2,1)S(1)} %get-tuple-element.15), channel_id=1, source_target_pairs={{0,4},{1,5},{2,6},{3,7},{4,8},{5,9},{6,10},{7,11},{8,12},{9,13},{1... | collective-permute-start | bytes 983048 | tf_op jit(solution)/shard_map/ppermute | solution.py:245
  7.2 6.9 %all-to-all-start = ((f32[32,2,512]{2,1,0:T(2,128)}), f32[32,2,512]{2,1,0:T(2,128)S(1)}, u32[]{:S(2)}, u32[]{:S(2)}) async-start(f32[32,2,512]{2,1,0:T(2,128)} %get-tuple-element.14), calls=%async_computation | async-start | bytes 262144 | tf_op jit(solution)/shard_map/all_to_all | solution.py:254
  14.1 0.1 pad_add_fusion.place
  14.2 0.0 copy-start.2
  14.2 0.0 copy-start.3
  14.2 0.0 copy-start.4
  14.2 0.0 collective-permute-done.prev
  14.2 0.0 copy-done.1
  14.2 0.9 %shard_map.57 = (bf16[10,40,512]{2,1,0:T(8,128)(2,1)}, bf16[10,40,512]{2,1,0:T(8,128)(2,1)}) custom-call(bf16[8,160,512]{2,1,0:T(8,128)(2,1)S(1)} %bitcast.8, bf16[2,160,512]{2,1,0:T(8,128)(2,1)S(1)} %collective-permute-done.prev), custom_call_target="tpu_custom_call" | custom-call | flops 10000000000 | bytes 209715200 | tf_op jit(solution)/shard_map/pallas_call | solution.py:85
  15.1 3.3 %collective-permute-start.1 = (bf16[10,40,512]{2,1,0:T(8,128)(2,1)}, bf16[10,40,512]{2,1,0:T(8,128)(2,1)S(1)}, u32[]{:S(2)}, u32[]{:S(2)}) collective-permute-start(bf16[10,40,512]{2,1,0:T(8,128)(2,1)} %get-tuple-element.17), channel_id=1, source_target_pairs={{0,1},{1,2},{2,3},{4,5},{5,6},{6,7},{8,9},{9,10},{10,11},{12,13},{... | collective-permute-start | bytes 1228808 | tf_op jit(solution)/shard_map/ppermute | solution.py:245
  18.4 1.3 %collective-permute-start.2 = (bf16[10,40,512]{2,1,0:T(8,128)(2,1)}, bf16[10,40,512]{2,1,0:T(8,128)(2,1)}, u32[]{:S(2)}, u32[]{:S(2)}) collective-permute-start(bf16[10,40,512]{2,1,0:T(8,128)(2,1)} %get-tuple-element.18), channel_id=1, source_target_pairs={{1,0},{2,1},{3,2},{5,4},{6,5},{7,6},{9,8},{10,9},{11,10},{13,12},{... | collective-permute-start | bytes 1228808 | tf_op jit(solution)/shard_map/ppermute | solution.py:245
  19.7 1.9 %all-to-all-done.pairs = f32[32,2,512]{2,1,0:T(2,128)S(1)} async-done(((f32[32,2,512]{2,1,0:T(2,128)}), f32[32,2,512]{2,1,0:T(2,128)S(1)}, u32[]{:S(2)}, u32[]{:S(2)}) %all-to-all-start) | async-done | bytes 131104 | tf_op jit(solution)/shard_map/all_to_all | solution.py:254
  21.7 0.0 copy-done.2
  21.7 0.0 copy-done.3
  21.7 0.0 copy-done.4
  21.7 12.0 %shard_map.56 = (bf16[8,80,512]{2,1,0:T(8,128)(2,1)S(1)}, bf16[10,80,512]{2,1,0:T(8,128)(2,1)S(1)}, bf16[10,80,512]{2,1,0:T(8,128)(2,1)S(1)}, f32[3,512]{1,0:T(4,128)S(1)}, bf16[9,3,512,512]{3,2,1,0:T(8,128)(2,1)S(1)}) custom-call(s32[2]{0:T(128)S(1)} %pad_add_fusion.place, f32[32,2,512]{2,1,0:T(2,128)S(1)} %all-to-all-done.pairs, f32[1,512]{1,0:T(1,128)S(1)} %bitcast.12, ...), custom_call_target="tpu_custom_call" | custom-call | flops 9059696640 | bytes 20971520 | tf_op jit(solution)/shard_map/pallas_call | solution.py:164
  33.7 0.0 collective-permute-done.1.up
  33.7 0.0 collective-permute-done.2.down
  33.7 11.6 %shard_map.58 = bf16[8,160,512]{2,1,0:T(8,128)(2,1)} custom-call(s32[2]{0:T(128)S(1)} %pad_add_fusion.place, f32[3,512]{1,0:T(4,128)S(1)} %get-tuple-element.16.coef, bf16[10,40,512]{2,1,0:T(8,128)(2,1)S(1)} %collective-permute-done.1.up, bf16[10,40,512]{2,1,0:T(8,128)(2,1)} %collective-permute-done.2.down, bf16[8,160,512]{2,1,0:T(8,128)(2,1)S(1)} %bitcast.11, ...), custom_call_target="tpu_custom_call" | custom-call | flops 9059696640 | bytes 20971520 | tf_op jit(solution)/shard_map/pallas_call | solution.py:220
Async XLA Ops:
  0.0 1.3 %copy-start = (bf16[8,4,40,512]{3,2,1,0:T(8,128)(2,1)S(1)}, bf16[8,4,40,512]{3,2,1,0:T(8,128)(2,1)}, u32[]{:S(2)}) copy-start(bf16[8,4,40,512]{3,2,1,0:T(8,128)(2,1)} %param.6) | copy-start | bytes 3932164
  1.3 12.9 %copy-start.1 = (bf16[8,4,40,512]{3,2,1,0:T(8,128)(2,1)S(1)}, bf16[8,4,40,512]{3,2,1,0:T(8,128)(2,1)}, u32[]{:S(2)}) copy-start(bf16[8,4,40,512]{3,2,1,0:T(8,128)(2,1)} %param.6) | copy-start | bytes 3932164
  2.7 11.5 %collective-permute-start = (bf16[2,160,512]{2,1,0:T(8,128)(2,1)S(1)}, bf16[2,160,512]{2,1,0:T(8,128)(2,1)S(1)}, u32[]{:S(2)}, u32[]{:S(2)}) collective-permute-start(bf16[2,160,512]{2,1,0:T(8,128)(2,1)S(1)} %get-tuple-element.15), channel_id=1, source_target_pairs={{0,4},{1,5},{2,6},{3,7},{4,8},{5,9},{6,10},{7,11},{8,12},{9,13},{1... | collective-permute-start | bytes 983048 | tf_op jit(solution)/shard_map/ppermute | solution.py:245
  7.2 14.5 %all-to-all-start = ((f32[32,2,512]{2,1,0:T(2,128)}), f32[32,2,512]{2,1,0:T(2,128)S(1)}, u32[]{:S(2)}, u32[]{:S(2)}) async-start(f32[32,2,512]{2,1,0:T(2,128)} %get-tuple-element.14), calls=%async_computation | async-start | bytes 262144 | tf_op jit(solution)/shard_map/all_to_all | solution.py:254
  14.2 7.5 %copy-start.2 = (bf16[8,4,40,512]{3,2,1,0:T(8,128)(2,1)S(1)}, bf16[8,4,40,512]{3,2,1,0:T(8,128)(2,1)}, u32[]{:S(2)}) copy-start(bf16[8,4,40,512]{3,2,1,0:T(8,128)(2,1)} %param.5) | copy-start | bytes 3932164
  14.2 7.5 %copy-start.3 = (f32[512]{0:T(512)S(1)}, f32[512]{0:T(512)}, u32[]{:S(2)}) copy-start(f32[512]{0:T(512)} %param.7) | copy-start | bytes 6148
  14.2 7.5 %copy-start.4 = (f32[512]{0:T(512)S(1)}, f32[512]{0:T(512)}, u32[]{:S(2)}) copy-start(f32[512]{0:T(512)} %param.8) | copy-start | bytes 6148
  15.1 18.6 %collective-permute-start.1 = (bf16[10,40,512]{2,1,0:T(8,128)(2,1)}, bf16[10,40,512]{2,1,0:T(8,128)(2,1)S(1)}, u32[]{:S(2)}, u32[]{:S(2)}) collective-permute-start(bf16[10,40,512]{2,1,0:T(8,128)(2,1)} %get-tuple-element.17), channel_id=1, source_target_pairs={{0,1},{1,2},{2,3},{4,5},{5,6},{6,7},{8,9},{9,10},{10,11},{12,13},{... | collective-permute-start | bytes 1228808 | tf_op jit(solution)/shard_map/ppermute | solution.py:245
  18.4 15.3 %collective-permute-start.2 = (bf16[10,40,512]{2,1,0:T(8,128)(2,1)}, bf16[10,40,512]{2,1,0:T(8,128)(2,1)}, u32[]{:S(2)}, u32[]{:S(2)}) collective-permute-start(bf16[10,40,512]{2,1,0:T(8,128)(2,1)} %get-tuple-element.18), channel_id=1, source_target_pairs={{1,0},{2,1},{3,2},{5,4},{6,5},{7,6},{9,8},{10,9},{11,10},{13,12},{... | collective-permute-start | bytes 1228808 | tf_op jit(solution)/shard_map/ppermute | solution.py:245

commit v3 on v2

--- a/solution.py
+++ b/solution.py
@@ -17,6 +17,8 @@
 BLOCK = 4
 ROW_SHARDS = 4
 WINDOW = 3
+CHUNKS = 4
+STATS_LIMIT = 63
 TAPS = 9
 VMEM = pl.BlockSpec(memory_space=pltpu.VMEM)
 
@@ -30,24 +32,35 @@
     return jax.ShapeDtypeStruct(shape, jnp.bfloat16)
 
 
-def stats_kernel(own, out, tail):
-    values = own[...].reshape(FRAMES * OWN, C).astype(jnp.float32)
-    mean = jnp.sum(values, axis=0, keepdims=True) * (1.0 / (FRAMES * OWN))
-    centered = own[...].reshape(FRAMES * OWN, C).astype(jnp.float32) - mean
-    spread = jnp.sum(centered * centered, axis=0, keepdims=True)
+def stats_kernel(own, out, tail, held, sems):
+    size = FRAMES // CHUNKS
+    parts = [slice(k * size, (k + 1) * size) for k in range(CHUNKS)]
+    copies = [pltpu.make_async_copy(own.at[part], held.at[part], sems.at[k]) for k, part in enumerate(parts)]
+    for copy in copies:
+        copy.start()
+    cells = size * OWN
+    means, spreads = [], []
+    for part, copy in zip(parts, copies):
+        copy.wait()
+        mean = jnp.sum(held[part].reshape(cells, C).astype(jnp.float32), axis=0, keepdims=True) * (1.0 / cells)
+        centered = held[part].reshape(cells, C).astype(jnp.float32) - mean
+        means.append(mean)
+        spreads.append(jnp.sum(centered * centered, axis=0, keepdims=True))
+    mean = sum(means) * (1.0 / CHUNKS)
+    spread = sum(spreads) + sum((each - mean) * (each - mean) for each in means) * float(cells)
     both = jnp.concatenate([mean, spread], axis=0)
     out[...] = jnp.broadcast_to(both[None], out.shape)
-    tail[...] = own[FRAMES - 2 :]
+    tail[...] = held[FRAMES - 2 :]
 
 
 def local_stats(own, copies):
     return pl.pallas_call(
         stats_kernel,
         out_shape=(jax.ShapeDtypeStruct((copies, 2, C), jnp.float32), bf16(2, OWN, C)),
-        in_specs=[VMEM],
+        in_specs=[HBM],
         out_specs=(VMEM, VMEM),
-        compiler_params=pltpu.CompilerParams(vmem_limit_bytes=8 * 2**20),
-        cost_estimate=pl.CostEstimate(flops=4 * 10**9, bytes_accessed=100 * 2**20, transcendentals=0),
+        scratch_shapes=[pltpu.VMEM((FRAMES, OWN, C), jnp.bfloat16), pltpu.SemaphoreType.DMA((CHUNKS,))],
+        compiler_params=pltpu.CompilerParams(vmem_limit_bytes=STATS_LIMIT * 2**20),
     )(own)
 
 
@@ -104,19 +117,22 @@
     for s in range(BLOCK + 2):
         frame(s)
     for t in range(0, FRAMES, BLOCK):
-        for p in range(3):
-            for q in range(3):
-                held = taps(3 * p + q, t == 0)
-                part = slab(t + p, q).reshape(cells, C)
-                for r in range(3):
-                    term = jnp.dot(part, held[r], preferred_element_type=jnp.float32)
-                    if p == 0 and q == 0:
-                        sums[r] = term
-                    else:
-                        sums[r] += term
-        left = jnp.where(column == 0, 0.0, pltpu.roll(sums[0], 1, 0))
-        right = jnp.where(column == COLS - 1, 0.0, pltpu.roll(sums[2], cells - 1, 0))
-        finish(t, (left + sums[1] + right).reshape(BLOCK, INNER, C))
+        held_sums = sums.at[t // BLOCK]
+        total = [None] * 3
+        for i in range(TAPS):
+            held = taps(i, t == 0)
+            part = slab(t + i // 3, i % 3).reshape(cells, C)
+            for r in range(3):
+                term = jnp.dot(part, held[r], preferred_element_type=jnp.float32)
+                if i == 0:
+                    held_sums[r] = term
+                elif i < TAPS - 1:
+                    held_sums[r] += term
+                else:
+                    total[r] = held_sums[r] + term
+        left = jnp.where(column == 0, 0.0, pltpu.roll(total[0], 1, 0))
+        right = jnp.where(column == COLS - 1, 0.0, pltpu.roll(total[2], cells - 1, 0))
+        finish(t, (left + total[1] + right).reshape(BLOCK, INNER, C))
         for s in range(t + BLOCK + 2, min(t + 2 * BLOCK + 2, WINDOWED)):
             frame(s)
 
@@ -174,7 +190,7 @@
         out_specs=(VMEM,) * 5,
         scratch_shapes=[
             pltpu.VMEM((WINDOWED, OWN, C), jnp.bfloat16),
-            pltpu.VMEM((3, BLOCK * INNER, C), jnp.float32),
+            pltpu.VMEM((FRAMES // BLOCK, 3, BLOCK * INNER, C), jnp.float32),
             pltpu.SemaphoreType.DMA((TAPS,)),
         ],
         compiler_params=pltpu.CompilerParams(vmem_limit_bytes=28 * 2**20),
@@ -184,7 +200,7 @@
     )(place, pairs, gain, bias, own, prev, latents, weight)
 
 
-def outer_kernel(place, coef, up, down, latents, inner, middle, ends, held, out, above_two, below_two, sums):
+def outer_kernel(place, coef, up, down, latents, inner, middle, ends, held, out, above_two, below_two, sums, done, sems):
     mean, scale, shift = coef[0:1], coef[1:2], coef[2:3]
     first = place[0] == 0
     keep_up = jnp.where(place[1] == 0, 0.0, 1.0)
@@ -211,9 +227,15 @@
         top = total[:, :COLS] + skip[:, :COLS]
         bottom = total[:, COLS:] + skip[:, 3 * COLS :]
         between = inner[t : t + BLOCK].astype(jnp.float32)
-        out[t : t + BLOCK] = jnp.concatenate([top, between, bottom], axis=1).astype(jnp.bfloat16)
+        done[t : t + BLOCK] = jnp.concatenate([top, between, bottom], axis=1).astype(jnp.bfloat16)
+        leave(t).start()
+
+    def leave(t):
+        return pltpu.make_async_copy(done.at[t : t + BLOCK], out.at[t : t + BLOCK], sems.at[t // BLOCK])
 
     accumulate(sums, taps, slab, frame, finish)
+    for t in range(0, FRAMES, BLOCK):
+        leave(t).wait()
 
 
 def outer_call(*operands):
@@ -221,11 +243,13 @@
         outer_kernel,
         out_shape=bf16(FRAMES, OWN, C),
         in_specs=[SMALL] + [VMEM] * 8,
-        out_specs=VMEM,
+        out_specs=HBM,
         scratch_shapes=[
             pltpu.VMEM((WINDOWED, INNER, C), jnp.bfloat16),
             pltpu.VMEM((WINDOWED, INNER, C), jnp.bfloat16),
-            pltpu.VMEM((3, BLOCK * INNER, C), jnp.float32),
+            pltpu.VMEM((FRAMES // BLOCK, 3, BLOCK * INNER, C), jnp.float32),
+            pltpu.VMEM((FRAMES, OWN, C), jnp.bfloat16),
+            pltpu.SemaphoreType.DMA((FRAMES // BLOCK,)),
         ],
         compiler_params=pltpu.CompilerParams(vmem_limit_bytes=26 * 2**20),
         cost_estimate=pl.CostEstimate(
@@ -234,15 +258,9 @@
     )(*operands)
 
 
-def send(block, by_frame, by_row):
-    frames, rows = lax.axis_size("frame"), lax.axis_size("row")
-    pairs = []
-    for f in range(frames):
-        for r in range(rows):
-            g, s = f + by_frame, r + by_row
-            if 0 <= g < frames and 0 <= s < rows:
-                pairs.append((f * rows + r, g * rows + s))
-    return lax.ppermute(block, ("frame", "row"), pairs)
+def send(block, axis, by):
+    size = lax.axis_size(axis)
+    return lax.ppermute(block, axis, [(i, (i + by) % size) for i in range(size)])
 
 
 def shards(latents, hidden, norm_gain, norm_bias, conv_weight):
@@ -250,11 +268,11 @@
     skip = latents.reshape(FRAMES, OWN, C)
     members = lax.axis_size("frame") * lax.axis_size("row")
     copies, last_two = local_stats(own, members)
-    prev = send(last_two, 1, 0)
+    prev = send(last_two, "frame", 1)
     pairs = lax.all_to_all(copies, ("frame", "row"), 0, 0, tiled=True)
     bottom, top = border_rows(own, prev)
-    up = send(bottom, 0, 1)
-    down = send(top, 0, -1)
+    up = send(bottom, "row", 1)
+    down = send(top, "row", -1)
     place = jnp.stack([lax.axis_index("frame"), lax.axis_index("row")]).astype(jnp.int32)
     gain, bias = norm_gain.reshape(1, C), norm_bias.reshape(1, C)
     inner, middle, ends, coef, held = inner_call(place, pairs, gain, bias, own, prev, skip, conv_weight)

time: 45.6 us -> 42.9 us (0.941)
  starting transfers between devices: 16 us -> 12.2 us
  waiting for transfers between devices: 1.93 us -> 2.56 us
  Pallas kernels: 25.9 us -> 26.4 us
    ppermute x3, starting transfers between devices: 9.09 us -> 5.29 us  [send(): lax.ppermute(block, axis, [(i, (i + by) % size) for i in range(size)])]
    pallas_call x1, Pallas kernels: 1.34 us -> 2.3 us  [local_stats(): pl.pallas_call(stats_kernel, out_shape=(jax.ShapeDtypeStruct((copies, 2,...]
    all_to_all x1, waiting for transfers between devices: 1.92 us -> 2.55 us  [shards(): pairs = lax.all_to_all(copies, ('frame', 'row'), 0, 0, tiled=True)]
  transfers between devices with their start and end apart: 4 -> 4, of which waited for: 1 -> 1; matrix products, arithmetic and copies ran while one was open for 0% -> 0% of each run, Pallas kernels for 29% -> 30%
where the time goes in v3:
time: 42.9 us; the launch traced here: 42.6 us
  Pallas kernels  26.4 us (62%)
  starting transfers between devices  12.2 us (28%)
  waiting for transfers between devices  2.56 us (6%)
  local copies, waits for them, and re-layouts  1.33 us (3%)
    pallas_call x1, Pallas kernels, inner_call(): pl.pallas_call(inner_kernel, out_shape=(bf16(FRAMES, INNER, C), bf16(WIND...  11.9 us
    pallas_call x1, Pallas kernels, outer_call(): pl.pallas_call(outer_kernel, out_shape=bf16(FRAMES, OWN, C), in_specs=[SM...  11.3 us
    all_to_all x1, starting transfers between devices, shards(): pairs = lax.all_to_all(copies, ('frame', 'row'), 0, 0, tiled=True)  6.91 us
    ppermute x3, starting transfers between devices, send(): lax.ppermute(block, axis, [(i, (i + by) % size) for i in range(size)])  5.29 us
    all_to_all x1, waiting for transfers between devices, shards(): pairs = lax.all_to_all(copies, ('frame', 'row'), 0, 0, tiled=True)  2.55 us
    pallas_call x1, Pallas kernels, local_stats(): pl.pallas_call(stats_kernel, out_shape=(jax.ShapeDtypeStruct((copies, 2,...  2.3 us
    unnamed x10, local copies, waits for them, and re-layouts  1.33 us
    pallas_call x1, Pallas kernels, border_rows(): pl.pallas_call(border_kernel, out_shape=(shape, shape), in_specs=[VMEM, V...  0.94 us
  transfers between devices with their start and end apart: 4, of which 1 were waited for; matrix products, arithmetic and copies ran while one was open for 0% of the time, Pallas kernels for 30%

profile of v3, /device:TPU:1, one launch (start us, length us, event | category | flops | bytes accessed | tf_op | source)
XLA Modules:
  0.0 42.6 jit_solution(11486180447331012623)
XLA Ops:
  0.0 2.3 %shard_map.55 = (f32[32,2,512]{2,1,0:T(2,128)}, bf16[2,160,512]{2,1,0:T(8,128)(2,1)}) custom-call(bf16[8,160,512]{2,1,0:T(8,128)(2,1)} %bitcast.7), custom_call_target="tpu_custom_call" | custom-call | tf_op jit(solution)/shard_map/pallas_call | solution.py:57
  2.3 2.6 %collective-permute-start = (bf16[2,160,512]{2,1,0:T(8,128)(2,1)}, bf16[2,160,512]{2,1,0:T(8,128)(2,1)S(1)}, u32[]{:S(2)}, u32[]{:S(2)}) collective-permute-start(bf16[2,160,512]{2,1,0:T(8,128)(2,1)} %get-tuple-element.15), channel_id=1, source_target_pairs={{0,4},{4,8},{8,12},{12,16},{16,20},{20,24},{24,28},{28,0},{1,5},{5... | collective-permute-start | bytes 983048 | tf_op jit(solution)/shard_map/ppermute | solution.py:263
  4.9 6.9 %all-to-all-start = ((f32[32,2,512]{2,1,0:T(2,128)}), f32[32,2,512]{2,1,0:T(2,128)S(1)}, u32[]{:S(2)}, u32[]{:S(2)}) async-start(f32[32,2,512]{2,1,0:T(2,128)} %get-tuple-element.14), calls=%async_computation | async-start | bytes 262144 | tf_op jit(solution)/shard_map/all_to_all | solution.py:272
  11.8 0.1 pad_add_fusion.place
  11.9 0.0 collective-permute-done.prev
  11.9 0.0 copy-start
  11.9 1.3 %copy-done = bf16[8,4,40,512]{3,2,1,0:T(8,128)(2,1)S(1)} copy-done((bf16[8,4,40,512]{3,2,1,0:T(8,128)(2,1)S(1)}, bf16[8,4,40,512]{3,2,1,0:T(8,128)(2,1)}, u32[]{:S(2)}) %copy-start) | copy-done | bytes 1310744
  13.2 0.0 copy-start.1
  13.2 0.0 copy-start.2
  13.2 0.0 copy-start.3
  13.2 0.0 copy-start.4
  13.2 0.9 %shard_map.57 = (bf16[10,40,512]{2,1,0:T(8,128)(2,1)}, bf16[10,40,512]{2,1,0:T(8,128)(2,1)}) custom-call(bf16[8,160,512]{2,1,0:T(8,128)(2,1)S(1)} %bitcast.8, bf16[2,160,512]{2,1,0:T(8,128)(2,1)S(1)} %collective-permute-done.prev), custom_call_target="tpu_custom_call" | custom-call | flops 10000000000 | bytes 209715200 | tf_op jit(solution)/shard_map/pallas_call | solution.py:98
  14.2 1.4 %collective-permute-start.1 = (bf16[10,40,512]{2,1,0:T(8,128)(2,1)}, bf16[10,40,512]{2,1,0:T(8,128)(2,1)S(1)}, u32[]{:S(2)}, u32[]{:S(2)}) collective-permute-start(bf16[10,40,512]{2,1,0:T(8,128)(2,1)} %get-tuple-element.17), channel_id=1, source_target_pairs={{0,1},{1,2},{2,3},{3,0},{4,5},{5,6},{6,7},{7,4},{8,9},{9,10},{10,1... | collective-permute-start | bytes 1228808 | tf_op jit(solution)/shard_map/ppermute | solution.py:263
  15.6 1.3 %collective-permute-start.2 = (bf16[10,40,512]{2,1,0:T(8,128)(2,1)}, bf16[10,40,512]{2,1,0:T(8,128)(2,1)}, u32[]{:S(2)}, u32[]{:S(2)}) collective-permute-start(bf16[10,40,512]{2,1,0:T(8,128)(2,1)} %get-tuple-element.18), channel_id=1, source_target_pairs={{0,3},{1,0},{2,1},{3,2},{4,7},{5,4},{6,5},{7,6},{8,11},{9,8},{10,9... | collective-permute-start | bytes 1228808 | tf_op jit(solution)/shard_map/ppermute | solution.py:263
  16.9 2.5 %all-to-all-done.pairs = f32[32,2,512]{2,1,0:T(2,128)S(1)} async-done(((f32[32,2,512]{2,1,0:T(2,128)}), f32[32,2,512]{2,1,0:T(2,128)S(1)}, u32[]{:S(2)}, u32[]{:S(2)}) %all-to-all-start) | async-done | bytes 131104 | tf_op jit(solution)/shard_map/all_to_all | solution.py:272
  19.4 0.0 copy-done.1
  19.4 0.0 copy-done.2
  19.4 0.0 copy-done.3
  19.4 0.0 copy-done.4
  19.4 11.9 %shard_map.56 = (bf16[8,80,512]{2,1,0:T(8,128)(2,1)S(1)}, bf16[10,80,512]{2,1,0:T(8,128)(2,1)S(1)}, bf16[10,80,512]{2,1,0:T(8,128)(2,1)S(1)}, f32[3,512]{1,0:T(4,128)S(1)}, bf16[9,3,512,512]{3,2,1,0:T(8,128)(2,1)S(1)}) custom-call(s32[2]{0:T(128)S(1)} %pad_add_fusion.place, f32[32,2,512]{2,1,0:T(2,128)S(1)} %all-to-all-done.pairs, f32[1,512]{1,0:T(1,128)S(1)} %bitcast.12, ...), custom_call_target="tpu_custom_call" | custom-call | flops 9059696640 | bytes 20971520 | tf_op jit(solution)/shard_map/pallas_call | solution.py:180
  31.3 0.0 collective-permute-done.1.up
  31.3 0.0 collective-permute-done.2.down
  31.3 11.3 %shard_map.58 = bf16[8,160,512]{2,1,0:T(8,128)(2,1)} custom-call(s32[2]{0:T(128)S(1)} %pad_add_fusion.place, f32[3,512]{1,0:T(4,128)S(1)} %get-tuple-element.16.coef, bf16[10,40,512]{2,1,0:T(8,128)(2,1)S(1)} %collective-permute-done.1.up, bf16[10,40,512]{2,1,0:T(8,128)(2,1)} %collective-permute-done.2.down, bf16[8,160,512]{2,1,0:T(8,128)(2,1)S(1)} %bitcast.11, ...), custom_call_target="tpu_custom_call" | custom-call | flops 9059696640 | bytes 20971520 | tf_op jit(solution)/shard_map/pallas_call | solution.py:242
Async XLA Ops:
  2.3 9.6 %collective-permute-start = (bf16[2,160,512]{2,1,0:T(8,128)(2,1)}, bf16[2,160,512]{2,1,0:T(8,128)(2,1)S(1)}, u32[]{:S(2)}, u32[]{:S(2)}) collective-permute-start(bf16[2,160,512]{2,1,0:T(8,128)(2,1)} %get-tuple-element.15), channel_id=1, source_target_pairs={{0,4},{4,8},{8,12},{12,16},{16,20},{20,24},{24,28},{28,0},{1,5},{5... | collective-permute-start | bytes 983048 | tf_op jit(solution)/shard_map/ppermute | solution.py:263
  4.9 14.5 %all-to-all-start = ((f32[32,2,512]{2,1,0:T(2,128)}), f32[32,2,512]{2,1,0:T(2,128)S(1)}, u32[]{:S(2)}, u32[]{:S(2)}) async-start(f32[32,2,512]{2,1,0:T(2,128)} %get-tuple-element.14), calls=%async_computation | async-start | bytes 262144 | tf_op jit(solution)/shard_map/all_to_all | solution.py:272
  11.9 1.3 %copy-start = (bf16[8,4,40,512]{3,2,1,0:T(8,128)(2,1)S(1)}, bf16[8,4,40,512]{3,2,1,0:T(8,128)(2,1)}, u32[]{:S(2)}) copy-start(bf16[8,4,40,512]{3,2,1,0:T(8,128)(2,1)} %param.6) | copy-start | bytes 3932164
  13.2 6.2 %copy-start.1 = (bf16[8,4,40,512]{3,2,1,0:T(8,128)(2,1)S(1)}, bf16[8,4,40,512]{3,2,1,0:T(8,128)(2,1)}, u32[]{:S(2)}) copy-start(bf16[8,4,40,512]{3,2,1,0:T(8,128)(2,1)} %param.6) | copy-start | bytes 3932164
  13.2 6.2 %copy-start.2 = (bf16[8,4,40,512]{3,2,1,0:T(8,128)(2,1)S(1)}, bf16[8,4,40,512]{3,2,1,0:T(8,128)(2,1)}, u32[]{:S(2)}) copy-start(bf16[8,4,40,512]{3,2,1,0:T(8,128)(2,1)} %param.5) | copy-start | bytes 3932164
  13.2 6.2 %copy-start.3 = (f32[512]{0:T(512)S(1)}, f32[512]{0:T(512)}, u32[]{:S(2)}) copy-start(f32[512]{0:T(512)} %param.7) | copy-start | bytes 6148
  13.2 6.2 %copy-start.4 = (f32[512]{0:T(512)S(1)}, f32[512]{0:T(512)}, u32[]{:S(2)}) copy-start(f32[512]{0:T(512)} %param.8) | copy-start | bytes 6148
  14.2 17.1 %collective-permute-start.1 = (bf16[10,40,512]{2,1,0:T(8,128)(2,1)}, bf16[10,40,512]{2,1,0:T(8,128)(2,1)S(1)}, u32[]{:S(2)}, u32[]{:S(2)}) collective-permute-start(bf16[10,40,512]{2,1,0:T(8,128)(2,1)} %get-tuple-element.17), channel_id=1, source_target_pairs={{0,1},{1,2},{2,3},{3,0},{4,5},{5,6},{6,7},{7,4},{8,9},{9,10},{10,1... | collective-permute-start | bytes 1228808 | tf_op jit(solution)/shard_map/ppermute | solution.py:263
  15.6 15.7 %collective-permute-start.2 = (bf16[10,40,512]{2,1,0:T(8,128)(2,1)}, bf16[10,40,512]{2,1,0:T(8,128)(2,1)}, u32[]{:S(2)}, u32[]{:S(2)}) collective-permute-start(bf16[10,40,512]{2,1,0:T(8,128)(2,1)} %get-tuple-element.18), channel_id=1, source_target_pairs={{0,3},{1,0},{2,1},{3,2},{4,7},{5,4},{6,5},{7,6},{8,11},{9,8},{10,9... | collective-permute-start | bytes 1228808 | tf_op jit(solution)/shard_map/ppermute | solution.py:263

commit v4 on v3

--- a/solution.py
+++ b/solution.py
@@ -18,6 +18,7 @@
 ROW_SHARDS = 4
 WINDOW = 3
 CHUNKS = 4
+PIECE = 2
 STATS_LIMIT = 63
 TAPS = 9
 VMEM = pl.BlockSpec(memory_space=pltpu.VMEM)
@@ -32,16 +33,19 @@
     return jax.ShapeDtypeStruct(shape, jnp.bfloat16)
 
 
-def stats_kernel(own, out, tail, held, sems):
+def stats_kernel(own, out, tail, held, sems, leave):
     size = FRAMES // CHUNKS
-    parts = [slice(k * size, (k + 1) * size) for k in range(CHUNKS)]
+    parts = [slice(k * size, (k + 1) * size) for k in reversed(range(CHUNKS))]
     copies = [pltpu.make_async_copy(own.at[part], held.at[part], sems.at[k]) for k, part in enumerate(parts)]
     for copy in copies:
         copy.start()
     cells = size * OWN
     means, spreads = [], []
-    for part, copy in zip(parts, copies):
+    last_two = pltpu.make_async_copy(held.at[FRAMES - 2 :], tail, leave.at[0])
+    for k, (part, copy) in enumerate(zip(parts, copies)):
         copy.wait()
+        if k == 0:
+            last_two.start()
         mean = jnp.sum(held[part].reshape(cells, C).astype(jnp.float32), axis=0, keepdims=True) * (1.0 / cells)
         centered = held[part].reshape(cells, C).astype(jnp.float32) - mean
         means.append(mean)
@@ -50,7 +54,7 @@
     spread = sum(spreads) + sum((each - mean) * (each - mean) for each in means) * float(cells)
     both = jnp.concatenate([mean, spread], axis=0)
     out[...] = jnp.broadcast_to(both[None], out.shape)
-    tail[...] = held[FRAMES - 2 :]
+    last_two.wait()
 
 
 def local_stats(own, copies):
@@ -58,8 +62,8 @@
         stats_kernel,
         out_shape=(jax.ShapeDtypeStruct((copies, 2, C), jnp.float32), bf16(2, OWN, C)),
         in_specs=[HBM],
-        out_specs=(VMEM, VMEM),
-        scratch_shapes=[pltpu.VMEM((FRAMES, OWN, C), jnp.bfloat16), pltpu.SemaphoreType.DMA((CHUNKS,))],
+        out_specs=(VMEM, HBM),
+        scratch_shapes=[pltpu.VMEM((FRAMES, OWN, C), jnp.bfloat16), pltpu.SemaphoreType.DMA((CHUNKS,)), pltpu.SemaphoreType.DMA((1,))],
         compiler_params=pltpu.CompilerParams(vmem_limit_bytes=STATS_LIMIT * 2**20),
     )(own)
 
@@ -223,19 +227,21 @@
         return (above_two, ends, below_two)[q][s : s + BLOCK]
 
     def finish(t, total):
-        skip = latents[t : t + BLOCK].astype(jnp.float32)
-        top = total[:, :COLS] + skip[:, :COLS]
-        bottom = total[:, COLS:] + skip[:, 3 * COLS :]
-        between = inner[t : t + BLOCK].astype(jnp.float32)
-        done[t : t + BLOCK] = jnp.concatenate([top, between, bottom], axis=1).astype(jnp.bfloat16)
-        leave(t).start()
-
-    def leave(t):
-        return pltpu.make_async_copy(done.at[t : t + BLOCK], out.at[t : t + BLOCK], sems.at[t // BLOCK])
+        for u in range(t, t + BLOCK, PIECE):
+            piece = total[u - t : u - t + PIECE]
+            skip = latents[u : u + PIECE].astype(jnp.float32)
+            top = piece[:, :COLS] + skip[:, :COLS]
+            bottom = piece[:, COLS:] + skip[:, 3 * COLS :]
+            between = inner[u : u + PIECE].astype(jnp.float32)
+            done[u : u + PIECE] = jnp.concatenate([top, between, bottom], axis=1).astype(jnp.bfloat16)
+            leave(u).start()
+
+    def leave(u):
+        return pltpu.make_async_copy(done.at[u : u + PIECE], out.at[u : u + PIECE], sems.at[u // PIECE])
 
     accumulate(sums, taps, slab, frame, finish)
-    for t in range(0, FRAMES, BLOCK):
-        leave(t).wait()
+    for u in range(0, FRAMES, PIECE):
+        leave(u).wait()
 
 
 def outer_call(*operands):
@@ -249,7 +255,7 @@
             pltpu.VMEM((WINDOWED, INNER, C), jnp.bfloat16),
             pltpu.VMEM((FRAMES // BLOCK, 3, BLOCK * INNER, C), jnp.float32),
             pltpu.VMEM((FRAMES, OWN, C), jnp.bfloat16),
-            pltpu.SemaphoreType.DMA((FRAMES // BLOCK,)),
+            pltpu.SemaphoreType.DMA((FRAMES // PIECE,)),
         ],
         compiler_params=pltpu.CompilerParams(vmem_limit_bytes=26 * 2**20),
         cost_estimate=pl.CostEstimate(

time: 42.9 us -> 43 us (level)
  no operation moved by 1% of the time
where the time goes in v4:
time: 43 us; the launch traced here: 42.7 us
  Pallas kernels  26.5 us (62%)
  starting transfers between devices  12.2 us (28%)
  waiting for transfers between devices  2.56 us (6%)
  local copies, waits for them, and re-layouts  1.33 us (3%)
    pallas_call x1, Pallas kernels, inner_call(): pl.pallas_call(inner_kernel, out_shape=(bf16(FRAMES, INNER, C), bf16(WIND...  11.9 us
    pallas_call x1, Pallas kernels, outer_call(): pl.pallas_call(outer_kernel, out_shape=bf16(FRAMES, OWN, C), in_specs=[SM...  11.3 us
    all_to_all x1, starting transfers between devices, shards(): pairs = lax.all_to_all(copies, ('frame', 'row'), 0, 0, tiled=True)  6.91 us
    ppermute x3, starting transfers between devices, send(): lax.ppermute(block, axis, [(i, (i + by) % size) for i in range(size)])  5.29 us
    all_to_all x1, waiting for transfers between devices, shards(): pairs = lax.all_to_all(copies, ('frame', 'row'), 0, 0, tiled=True)  2.55 us
    pallas_call x1, Pallas kernels, local_stats(): pl.pallas_call(stats_kernel, out_shape=(jax.ShapeDtypeStruct((copies, 2,...  2.38 us
    unnamed x10, local copies, waits for them, and re-layouts  1.33 us
    pallas_call x1, Pallas kernels, border_rows(): pl.pallas_call(border_kernel, out_shape=(shape, shape), in_specs=[VMEM, V...  0.94 us
  transfers between devices with their start and end apart: 4, of which 1 were waited for; matrix products, arithmetic and copies ran while one was open for 0% of the time, Pallas kernels for 30%

profile of v4, /device:TPU:1, one launch (start us, length us, event | category | flops | bytes accessed | tf_op | source)
XLA Modules:
  0.0 42.7 jit_solution(6312753618453524471)
XLA Ops:
  0.0 2.4 %shard_map.55 = (f32[32,2,512]{2,1,0:T(2,128)}, bf16[2,160,512]{2,1,0:T(8,128)(2,1)}) custom-call(bf16[8,160,512]{2,1,0:T(8,128)(2,1)} %bitcast.7), custom_call_target="tpu_custom_call" | custom-call | tf_op jit(solution)/shard_map/pallas_call | solution.py:61
  2.4 2.6 %collective-permute-start = (bf16[2,160,512]{2,1,0:T(8,128)(2,1)}, bf16[2,160,512]{2,1,0:T(8,128)(2,1)S(1)}, u32[]{:S(2)}, u32[]{:S(2)}) collective-permute-start(bf16[2,160,512]{2,1,0:T(8,128)(2,1)} %get-tuple-element.15), channel_id=1, source_target_pairs={{0,4},{4,8},{8,12},{12,16},{16,20},{20,24},{24,28},{28,0},{1,5},{5... | collective-permute-start | bytes 983048 | tf_op jit(solution)/shard_map/ppermute | solution.py:269
  5.0 6.9 %all-to-all-start = ((f32[32,2,512]{2,1,0:T(2,128)}), f32[32,2,512]{2,1,0:T(2,128)S(1)}, u32[]{:S(2)}, u32[]{:S(2)}) async-start(f32[32,2,512]{2,1,0:T(2,128)} %get-tuple-element.14), calls=%async_computation | async-start | bytes 262144 | tf_op jit(solution)/shard_map/all_to_all | solution.py:278
  11.9 0.1 pad_add_fusion.place
  12.0 0.0 collective-permute-done.prev
  12.0 0.0 copy-start
  12.0 1.3 %copy-done = bf16[8,4,40,512]{3,2,1,0:T(8,128)(2,1)S(1)} copy-done((bf16[8,4,40,512]{3,2,1,0:T(8,128)(2,1)S(1)}, bf16[8,4,40,512]{3,2,1,0:T(8,128)(2,1)}, u32[]{:S(2)}) %copy-start) | copy-done | bytes 1310744
  13.3 0.0 copy-start.1
  13.3 0.0 copy-start.2
  13.3 0.0 copy-start.3
  13.3 0.0 copy-start.4
  13.3 0.9 %shard_map.57 = (bf16[10,40,512]{2,1,0:T(8,128)(2,1)}, bf16[10,40,512]{2,1,0:T(8,128)(2,1)}) custom-call(bf16[8,160,512]{2,1,0:T(8,128)(2,1)S(1)} %bitcast.8, bf16[2,160,512]{2,1,0:T(8,128)(2,1)S(1)} %collective-permute-done.prev), custom_call_target="tpu_custom_call" | custom-call | flops 10000000000 | bytes 209715200 | tf_op jit(solution)/shard_map/pallas_call | solution.py:102
  14.3 1.4 %collective-permute-start.1 = (bf16[10,40,512]{2,1,0:T(8,128)(2,1)}, bf16[10,40,512]{2,1,0:T(8,128)(2,1)S(1)}, u32[]{:S(2)}, u32[]{:S(2)}) collective-permute-start(bf16[10,40,512]{2,1,0:T(8,128)(2,1)} %get-tuple-element.17), channel_id=1, source_target_pairs={{0,1},{1,2},{2,3},{3,0},{4,5},{5,6},{6,7},{7,4},{8,9},{9,10},{10,1... | collective-permute-start | bytes 1228808 | tf_op jit(solution)/shard_map/ppermute | solution.py:269
  15.7 1.3 %collective-permute-start.2 = (bf16[10,40,512]{2,1,0:T(8,128)(2,1)}, bf16[10,40,512]{2,1,0:T(8,128)(2,1)}, u32[]{:S(2)}, u32[]{:S(2)}) collective-permute-start(bf16[10,40,512]{2,1,0:T(8,128)(2,1)} %get-tuple-element.18), channel_id=1, source_target_pairs={{0,3},{1,0},{2,1},{3,2},{4,7},{5,4},{6,5},{7,6},{8,11},{9,8},{10,9... | collective-permute-start | bytes 1228808 | tf_op jit(solution)/shard_map/ppermute | solution.py:269
  16.9 2.5 %all-to-all-done.pairs = f32[32,2,512]{2,1,0:T(2,128)S(1)} async-done(((f32[32,2,512]{2,1,0:T(2,128)}), f32[32,2,512]{2,1,0:T(2,128)S(1)}, u32[]{:S(2)}, u32[]{:S(2)}) %all-to-all-start) | async-done | bytes 131104 | tf_op jit(solution)/shard_map/all_to_all | solution.py:278
  19.5 0.0 copy-done.1
  19.5 0.0 copy-done.2
  19.5 0.0 copy-done.3
  19.5 0.0 copy-done.4
  19.5 11.9 %shard_map.56 = (bf16[8,80,512]{2,1,0:T(8,128)(2,1)S(1)}, bf16[10,80,512]{2,1,0:T(8,128)(2,1)S(1)}, bf16[10,80,512]{2,1,0:T(8,128)(2,1)S(1)}, f32[3,512]{1,0:T(4,128)S(1)}, bf16[9,3,512,512]{3,2,1,0:T(8,128)(2,1)S(1)}) custom-call(s32[2]{0:T(128)S(1)} %pad_add_fusion.place, f32[32,2,512]{2,1,0:T(2,128)S(1)} %all-to-all-done.pairs, f32[1,512]{1,0:T(1,128)S(1)} %bitcast.12, ...), custom_call_target="tpu_custom_call" | custom-call | flops 9059696640 | bytes 20971520 | tf_op jit(solution)/shard_map/pallas_call | solution.py:184
  31.4 0.0 collective-permute-done.1.up
  31.4 0.0 collective-permute-done.2.down
  31.4 11.3 %shard_map.58 = bf16[8,160,512]{2,1,0:T(8,128)(2,1)} custom-call(s32[2]{0:T(128)S(1)} %pad_add_fusion.place, f32[3,512]{1,0:T(4,128)S(1)} %get-tuple-element.16.coef, bf16[10,40,512]{2,1,0:T(8,128)(2,1)S(1)} %collective-permute-done.1.up, bf16[10,40,512]{2,1,0:T(8,128)(2,1)} %collective-permute-done.2.down, bf16[8,160,512]{2,1,0:T(8,128)(2,1)S(1)} %bitcast.11, ...), custom_call_target="tpu_custom_call" | custom-call | flops 9059696640 | bytes 20971520 | tf_op jit(solution)/shard_map/pallas_call | solution.py:248
Async XLA Ops:
  2.4 9.6 %collective-permute-start = (bf16[2,160,512]{2,1,0:T(8,128)(2,1)}, bf16[2,160,512]{2,1,0:T(8,128)(2,1)S(1)}, u32[]{:S(2)}, u32[]{:S(2)}) collective-permute-start(bf16[2,160,512]{2,1,0:T(8,128)(2,1)} %get-tuple-element.15), channel_id=1, source_target_pairs={{0,4},{4,8},{8,12},{12,16},{16,20},{20,24},{24,28},{28,0},{1,5},{5... | collective-permute-start | bytes 983048 | tf_op jit(solution)/shard_map/ppermute | solution.py:269
  5.0 14.5 %all-to-all-start = ((f32[32,2,512]{2,1,0:T(2,128)}), f32[32,2,512]{2,1,0:T(2,128)S(1)}, u32[]{:S(2)}, u32[]{:S(2)}) async-start(f32[32,2,512]{2,1,0:T(2,128)} %get-tuple-element.14), calls=%async_computation | async-start | bytes 262144 | tf_op jit(solution)/shard_map/all_to_all | solution.py:278
  12.0 1.3 %copy-start = (bf16[8,4,40,512]{3,2,1,0:T(8,128)(2,1)S(1)}, bf16[8,4,40,512]{3,2,1,0:T(8,128)(2,1)}, u32[]{:S(2)}) copy-start(bf16[8,4,40,512]{3,2,1,0:T(8,128)(2,1)} %param.6) | copy-start | bytes 3932164
  13.3 6.2 %copy-start.1 = (bf16[8,4,40,512]{3,2,1,0:T(8,128)(2,1)S(1)}, bf16[8,4,40,512]{3,2,1,0:T(8,128)(2,1)}, u32[]{:S(2)}) copy-start(bf16[8,4,40,512]{3,2,1,0:T(8,128)(2,1)} %param.6) | copy-start | bytes 3932164
  13.3 6.2 %copy-start.2 = (bf16[8,4,40,512]{3,2,1,0:T(8,128)(2,1)S(1)}, bf16[8,4,40,512]{3,2,1,0:T(8,128)(2,1)}, u32[]{:S(2)}) copy-start(bf16[8,4,40,512]{3,2,1,0:T(8,128)(2,1)} %param.5) | copy-start | bytes 3932164
  13.3 6.2 %copy-start.3 = (f32[512]{0:T(512)S(1)}, f32[512]{0:T(512)}, u32[]{:S(2)}) copy-start(f32[512]{0:T(512)} %param.7) | copy-start | bytes 6148
  13.3 6.2 %copy-start.4 = (f32[512]{0:T(512)S(1)}, f32[512]{0:T(512)}, u32[]{:S(2)}) copy-start(f32[512]{0:T(512)} %param.8) | copy-start | bytes 6148
  14.3 17.1 %collective-permute-start.1 = (bf16[10,40,512]{2,1,0:T(8,128)(2,1)}, bf16[10,40,512]{2,1,0:T(8,128)(2,1)S(1)}, u32[]{:S(2)}, u32[]{:S(2)}) collective-permute-start(bf16[10,40,512]{2,1,0:T(8,128)(2,1)} %get-tuple-element.17), channel_id=1, source_target_pairs={{0,1},{1,2},{2,3},{3,0},{4,5},{5,6},{6,7},{7,4},{8,9},{9,10},{10,1... | collective-permute-start | bytes 1228808 | tf_op jit(solution)/shard_map/ppermute | solution.py:269
  15.7 15.7 %collective-permute-start.2 = (bf16[10,40,512]{2,1,0:T(8,128)(2,1)}, bf16[10,40,512]{2,1,0:T(8,128)(2,1)}, u32[]{:S(2)}, u32[]{:S(2)}) collective-permute-start(bf16[10,40,512]{2,1,0:T(8,128)(2,1)} %get-tuple-element.18), channel_id=1, source_target_pairs={{0,3},{1,0},{2,1},{3,2},{4,7},{5,4},{6,5},{7,6},{8,11},{9,8},{10,9... | collective-permute-start | bytes 1228808 | tf_op jit(solution)/shard_map/ppermute | solution.py:269

commit v5 on v4

--- a/solution.py
+++ b/solution.py
@@ -124,10 +124,9 @@
         held_sums = sums.at[t // BLOCK]
         total = [None] * 3
         for i in range(TAPS):
-            held = taps(i, t == 0)
             part = slab(t + i // 3, i % 3).reshape(cells, C)
             for r in range(3):
-                term = jnp.dot(part, held[r], preferred_element_type=jnp.float32)
+                term = jnp.dot(part, taps(i, r, t == 0), preferred_element_type=jnp.float32)
                 if i == 0:
                     held_sums[r] = term
                 elif i < TAPS - 1:
@@ -143,10 +142,10 @@
 
 def inner_kernel(place, pairs, gain, bias, own, prev, latents, weight, out, middle, ends, coef, held, tall, sums, sems):
     copies = [
-        pltpu.make_async_copy(weight.at[i // 3, i % 3], held.at[i], sems.at[i])
-        for i in range(TAPS)
+        pltpu.make_async_copy(weight.at[i // 9, i // 3 % 3, i % 3], held.at[i // 3, i % 3], sems.at[i])
+        for i in range(3 * TAPS)
     ]
-    for copy in copies[:WINDOW]:
+    for copy in copies[: 3 * WINDOW]:
         copy.start()
     mean, variance = merge_stats(pairs[...])
     scale = gain[...] / jnp.sqrt(variance + 1e-06)
@@ -154,12 +153,13 @@
     coef[...] = jnp.concatenate([mean, scale, shift], axis=0)
     first = place[0] == 0
 
-    def taps(i, once):
+    def taps(i, r, once):
         if once:
-            copies[i].wait()
-            if i + WINDOW < TAPS:
-                copies[i + WINDOW].start()
-        return held.at[i]
+            j = 3 * i + r
+            copies[j].wait()
+            if j + 3 * WINDOW < 3 * TAPS:
+                copies[j + 3 * WINDOW].start()
+        return held[i, r]
 
     def frame(s):
         values = jnp.where(first, own[0], prev[s]) if s < 2 else own[s - 2]
@@ -195,7 +195,7 @@
         scratch_shapes=[
             pltpu.VMEM((WINDOWED, OWN, C), jnp.bfloat16),
             pltpu.VMEM((FRAMES // BLOCK, 3, BLOCK * INNER, C), jnp.float32),
-            pltpu.SemaphoreType.DMA((TAPS,)),
+            pltpu.SemaphoreType.DMA((3 * TAPS,)),
         ],
         compiler_params=pltpu.CompilerParams(vmem_limit_bytes=28 * 2**20),
         cost_estimate=pl.CostEstimate(
@@ -210,8 +210,8 @@
     keep_up = jnp.where(place[1] == 0, 0.0, 1.0)
     keep_down = jnp.where(place[1] == ROW_SHARDS - 1, 0.0, 1.0)
 
-    def taps(i, once):
-        return held.at[i]
+    def taps(i, r, once):
+        return held[i, r]
 
     def frame(s):
         above, below = up[s], down[s]

time: 43 us -> 44.2 us (1.028)
  Pallas kernels: 26.5 us -> 27.7 us
    pallas_call x1, Pallas kernels: 11.9 us -> 13.1 us  [inner_call(): pl.pallas_call(inner_kernel, out_shape=(bf16(FRAMES, INNER, C), bf16(WIND...]
  transfers between devices with their start and end apart: 4 -> 4, of which waited for: 1 -> 1; matrix products, arithmetic and copies ran while one was open for 0% -> 0% of each run, Pallas kernels for 30% -> 32%
where the time goes in v5:
time: 44.2 us; the launch traced here: 43.9 us
  Pallas kernels  27.7 us (63%)
  starting transfers between devices  12.2 us (28%)
  waiting for transfers between devices  2.56 us (6%)
  local copies, waits for them, and re-layouts  1.33 us (3%)
    pallas_call x1, Pallas kernels, inner_call(): pl.pallas_call(inner_kernel, out_shape=(bf16(FRAMES, INNER, C), bf16(WIND...  13.1 us
    pallas_call x1, Pallas kernels, outer_call(): pl.pallas_call(outer_kernel, out_shape=bf16(FRAMES, OWN, C), in_specs=[SM...  11.3 us
    all_to_all x1, starting transfers between devices, shards(): pairs = lax.all_to_all(copies, ('frame', 'row'), 0, 0, tiled=True)  6.91 us
    ppermute x3, starting transfers between devices, send(): lax.ppermute(block, axis, [(i, (i + by) % size) for i in range(size)])  5.29 us
    all_to_all x1, waiting for transfers between devices, shards(): pairs = lax.all_to_all(copies, ('frame', 'row'), 0, 0, tiled=True)  2.55 us
    pallas_call x1, Pallas kernels, local_stats(): pl.pallas_call(stats_kernel, out_shape=(jax.ShapeDtypeStruct((copies, 2,...  2.38 us
    unnamed x10, local copies, waits for them, and re-layouts  1.33 us
    pallas_call x1, Pallas kernels, border_rows(): pl.pallas_call(border_kernel, out_shape=(shape, shape), in_specs=[VMEM, V...  0.94 us
  transfers between devices with their start and end apart: 4, of which 1 were waited for; matrix products, arithmetic and copies ran while one was open for 0% of the time, Pallas kernels for 32%

profile of v5, /device:TPU:1, one launch (start us, length us, event | category | flops | bytes accessed | tf_op | source)
XLA Modules:
  0.0 43.9 jit_solution(17440831756095874863)
XLA Ops:
  0.0 2.4 %shard_map.55 = (f32[32,2,512]{2,1,0:T(2,128)}, bf16[2,160,512]{2,1,0:T(8,128)(2,1)}) custom-call(bf16[8,160,512]{2,1,0:T(8,128)(2,1)} %bitcast.7), custom_call_target="tpu_custom_call" | custom-call | tf_op jit(solution)/shard_map/pallas_call | solution.py:61
  2.4 2.6 %collective-permute-start = (bf16[2,160,512]{2,1,0:T(8,128)(2,1)}, bf16[2,160,512]{2,1,0:T(8,128)(2,1)S(1)}, u32[]{:S(2)}, u32[]{:S(2)}) collective-permute-start(bf16[2,160,512]{2,1,0:T(8,128)(2,1)} %get-tuple-element.15), channel_id=1, source_target_pairs={{0,4},{4,8},{8,12},{12,16},{16,20},{20,24},{24,28},{28,0},{1,5},{5... | collective-permute-start | bytes 983048 | tf_op jit(solution)/shard_map/ppermute | solution.py:269
  5.0 6.9 %all-to-all-start = ((f32[32,2,512]{2,1,0:T(2,128)}), f32[32,2,512]{2,1,0:T(2,128)S(1)}, u32[]{:S(2)}, u32[]{:S(2)}) async-start(f32[32,2,512]{2,1,0:T(2,128)} %get-tuple-element.14), calls=%async_computation | async-start | bytes 262144 | tf_op jit(solution)/shard_map/all_to_all | solution.py:278
  11.9 0.1 pad_add_fusion.place
  12.0 0.0 collective-permute-done.prev
  12.0 0.0 copy-start
  12.0 1.3 %copy-done = bf16[8,4,40,512]{3,2,1,0:T(8,128)(2,1)S(1)} copy-done((bf16[8,4,40,512]{3,2,1,0:T(8,128)(2,1)S(1)}, bf16[8,4,40,512]{3,2,1,0:T(8,128)(2,1)}, u32[]{:S(2)}) %copy-start) | copy-done | bytes 1310744
  13.3 0.0 copy-start.1
  13.3 0.0 copy-start.2
  13.3 0.0 copy-start.3
  13.3 0.0 copy-start.4
  13.3 0.9 %shard_map.57 = (bf16[10,40,512]{2,1,0:T(8,128)(2,1)}, bf16[10,40,512]{2,1,0:T(8,128)(2,1)}) custom-call(bf16[8,160,512]{2,1,0:T(8,128)(2,1)S(1)} %bitcast.8, bf16[2,160,512]{2,1,0:T(8,128)(2,1)S(1)} %collective-permute-done.prev), custom_call_target="tpu_custom_call" | custom-call | flops 10000000000 | bytes 209715200 | tf_op jit(solution)/shard_map/pallas_call | solution.py:102
  14.3 1.4 %collective-permute-start.1 = (bf16[10,40,512]{2,1,0:T(8,128)(2,1)}, bf16[10,40,512]{2,1,0:T(8,128)(2,1)S(1)}, u32[]{:S(2)}, u32[]{:S(2)}) collective-permute-start(bf16[10,40,512]{2,1,0:T(8,128)(2,1)} %get-tuple-element.17), channel_id=1, source_target_pairs={{0,1},{1,2},{2,3},{3,0},{4,5},{5,6},{6,7},{7,4},{8,9},{9,10},{10,1... | collective-permute-start | bytes 1228808 | tf_op jit(solution)/shard_map/ppermute | solution.py:269
  15.7 1.3 %collective-permute-start.2 = (bf16[10,40,512]{2,1,0:T(8,128)(2,1)}, bf16[10,40,512]{2,1,0:T(8,128)(2,1)}, u32[]{:S(2)}, u32[]{:S(2)}) collective-permute-start(bf16[10,40,512]{2,1,0:T(8,128)(2,1)} %get-tuple-element.18), channel_id=1, source_target_pairs={{0,3},{1,0},{2,1},{3,2},{4,7},{5,4},{6,5},{7,6},{8,11},{9,8},{10,9... | collective-permute-start | bytes 1228808 | tf_op jit(solution)/shard_map/ppermute | solution.py:269
  16.9 2.5 %all-to-all-done.pairs = f32[32,2,512]{2,1,0:T(2,128)S(1)} async-done(((f32[32,2,512]{2,1,0:T(2,128)}), f32[32,2,512]{2,1,0:T(2,128)S(1)}, u32[]{:S(2)}, u32[]{:S(2)}) %all-to-all-start) | async-done | bytes 131104 | tf_op jit(solution)/shard_map/all_to_all | solution.py:278
  19.5 0.0 copy-done.1
  19.5 0.0 copy-done.2
  19.5 0.0 copy-done.3
  19.5 0.0 copy-done.4
  19.5 13.1 %shard_map.56 = (bf16[8,80,512]{2,1,0:T(8,128)(2,1)S(1)}, bf16[10,80,512]{2,1,0:T(8,128)(2,1)S(1)}, bf16[10,80,512]{2,1,0:T(8,128)(2,1)S(1)}, f32[3,512]{1,0:T(4,128)S(1)}, bf16[9,3,512,512]{3,2,1,0:T(8,128)(2,1)S(1)}) custom-call(s32[2]{0:T(128)S(1)} %pad_add_fusion.place, f32[32,2,512]{2,1,0:T(2,128)S(1)} %all-to-all-done.pairs, f32[1,512]{1,0:T(1,128)S(1)} %bitcast.12, ...), custom_call_target="tpu_custom_call" | custom-call | flops 9059696640 | bytes 20971520 | tf_op jit(solution)/shard_map/pallas_call | solution.py:184
  32.6 0.0 collective-permute-done.1.up
  32.6 0.0 collective-permute-done.2.down
  32.6 11.3 %shard_map.58 = bf16[8,160,512]{2,1,0:T(8,128)(2,1)} custom-call(s32[2]{0:T(128)S(1)} %pad_add_fusion.place, f32[3,512]{1,0:T(4,128)S(1)} %get-tuple-element.16.coef, bf16[10,40,512]{2,1,0:T(8,128)(2,1)S(1)} %collective-permute-done.1.up, bf16[10,40,512]{2,1,0:T(8,128)(2,1)} %collective-permute-done.2.down, bf16[8,160,512]{2,1,0:T(8,128)(2,1)S(1)} %bitcast.11, ...), custom_call_target="tpu_custom_call" | custom-call | flops 9059696640 | bytes 20971520 | tf_op jit(solution)/shard_map/pallas_call | solution.py:248
Async XLA Ops:
  2.4 9.6 %collective-permute-start = (bf16[2,160,512]{2,1,0:T(8,128)(2,1)}, bf16[2,160,512]{2,1,0:T(8,128)(2,1)S(1)}, u32[]{:S(2)}, u32[]{:S(2)}) collective-permute-start(bf16[2,160,512]{2,1,0:T(8,128)(2,1)} %get-tuple-element.15), channel_id=1, source_target_pairs={{0,4},{4,8},{8,12},{12,16},{16,20},{20,24},{24,28},{28,0},{1,5},{5... | collective-permute-start | bytes 983048 | tf_op jit(solution)/shard_map/ppermute | solution.py:269
  5.0 14.5 %all-to-all-start = ((f32[32,2,512]{2,1,0:T(2,128)}), f32[32,2,512]{2,1,0:T(2,128)S(1)}, u32[]{:S(2)}, u32[]{:S(2)}) async-start(f32[32,2,512]{2,1,0:T(2,128)} %get-tuple-element.14), calls=%async_computation | async-start | bytes 262144 | tf_op jit(solution)/shard_map/all_to_all | solution.py:278
  12.0 1.3 %copy-start = (bf16[8,4,40,512]{3,2,1,0:T(8,128)(2,1)S(1)}, bf16[8,4,40,512]{3,2,1,0:T(8,128)(2,1)}, u32[]{:S(2)}) copy-start(bf16[8,4,40,512]{3,2,1,0:T(8,128)(2,1)} %param.6) | copy-start | bytes 3932164
  13.3 6.2 %copy-start.1 = (bf16[8,4,40,512]{3,2,1,0:T(8,128)(2,1)S(1)}, bf16[8,4,40,512]{3,2,1,0:T(8,128)(2,1)}, u32[]{:S(2)}) copy-start(bf16[8,4,40,512]{3,2,1,0:T(8,128)(2,1)} %param.6) | copy-start | bytes 3932164
  13.3 6.2 %copy-start.2 = (bf16[8,4,40,512]{3,2,1,0:T(8,128)(2,1)S(1)}, bf16[8,4,40,512]{3,2,1,0:T(8,128)(2,1)}, u32[]{:S(2)}) copy-start(bf16[8,4,40,512]{3,2,1,0:T(8,128)(2,1)} %param.5) | copy-start | bytes 3932164
  13.3 6.2 %copy-start.3 = (f32[512]{0:T(512)S(1)}, f32[512]{0:T(512)}, u32[]{:S(2)}) copy-start(f32[512]{0:T(512)} %param.7) | copy-start | bytes 6148
  13.3 6.2 %copy-start.4 = (f32[512]{0:T(512)S(1)}, f32[512]{0:T(512)}, u32[]{:S(2)}) copy-start(f32[512]{0:T(512)} %param.8) | copy-start | bytes 6148
  14.3 18.3 %collective-permute-start.1 = (bf16[10,40,512]{2,1,0:T(8,128)(2,1)}, bf16[10,40,512]{2,1,0:T(8,128)(2,1)S(1)}, u32[]{:S(2)}, u32[]{:S(2)}) collective-permute-start(bf16[10,40,512]{2,1,0:T(8,128)(2,1)} %get-tuple-element.17), channel_id=1, source_target_pairs={{0,1},{1,2},{2,3},{3,0},{4,5},{5,6},{6,7},{7,4},{8,9},{9,10},{10,1... | collective-permute-start | bytes 1228808 | tf_op jit(solution)/shard_map/ppermute | solution.py:269
  15.7 17.0 %collective-permute-start.2 = (bf16[10,40,512]{2,1,0:T(8,128)(2,1)}, bf16[10,40,512]{2,1,0:T(8,128)(2,1)}, u32[]{:S(2)}, u32[]{:S(2)}) collective-permute-start(bf16[10,40,512]{2,1,0:T(8,128)(2,1)} %get-tuple-element.18), channel_id=1, source_target_pairs={{0,3},{1,0},{2,1},{3,2},{4,7},{5,4},{6,5},{7,6},{8,11},{9,8},{10,9... | collective-permute-start | bytes 1228808 | tf_op jit(solution)/shard_map/ppermute | solution.py:269
